TPU v7x, 512 devices: a whole 4x4x16 slice. The times are simulated.
512 devices in a mesh: blk: 128 (over x, y_lo, z), grp: 4 (over y_hi, core).
Axes of the slice: x: 4, y: 4 (y_hi: 2, y_lo: 2; y = y_hi * 2 + y_lo), z: 16, core: 2. Of those that a mesh axis runs over, the one named last changes fastest.
Arguments:
- amplitudes: bfloat16 [128, 512, 1024], P('blk', None, 'grp'), may hold values from -6 to 6
- integrals: bfloat16 [1024, 1024, 1024], P('blk', 'grp'), may hold values from -0.1875 to 0.1875
- cd_index: int32 [1024], replicated, may hold values from 0 to 127, as said below
- live_blocks: int32 [128], replicated, may hold values from 4 to 8, as said below
- occ_energy: float32 [512], P('grp'), may hold values from -3 to -0.5
- vir_energy: float32 [128, 1024], P('blk'), may hold values from 0.5 to 4
Outputs:
- amplitude_step: float32 [128, 512, 1024], P('blk', 'grp')
Inputs may be any that keep to these rules, and one draw needn't show every extreme that they name: (cd_index[k] - k // 8) mod 128 is at most 2 or at least 126; among the first 4 slots of each pair block every nonzero offset from -2 to 2 occurs once. `live_blocks`: 8 is reached by some pair block in every draw.
All inputs are finite; a program needn't handle non-finite values.
Results may differ from a plain program's by a relative error of at most 0.0003.
Values may be sent and summed in bfloat16 or wider, within the bound.
No kernel may reach another device: no remote copies, remote signals or barrier semaphores. Data moves between devices by JAX's collectives and lax.ppermute only.
A program may use at most 64 MiB of HBM per device.

v0:
```python
import jax
import jax.numpy as jnp
from jax import lax
from jax.sharding import PartitionSpec as P

REACH = 2


def shifted(value, axis, steps):
    count = lax.axis_size(axis)
    pairs = [(source, (source + steps) % count) for source in range(count)]
    return lax.ppermute(value, axis, pairs)


def cut_along(value, dim, devices):
    shape = value.shape
    tiles = value.reshape(*shape[:dim], devices, shape[dim] // devices, *shape[dim + 1 :])
    return jnp.moveaxis(tiles, dim, 0)


def sum_at_owner(value, axis, dim):
    tiles = cut_along(value, dim, lax.axis_size(axis))
    arrived = lax.all_to_all(tiles, axis, split_axis=0, concat_axis=0, tiled=True)
    return arrived.sum(axis=0)


def cycle_offsets(cd_values, center, cycle_reach, cycle_size):
    return jnp.mod(cd_values - center + cycle_reach, cycle_size)


def contract_tasks(nearby, pieces, offsets, begin_slot, end_slot):
    row_count = nearby.shape[1]
    col_count = pieces.shape[2]

    def one_task(slot_index, running):
        amp_block = nearby[offsets[slot_index]]
        return running + jnp.dot(amp_block, pieces[slot_index], preferred_element_type=jnp.float32)

    start_sum = jnp.zeros((row_count, col_count), jnp.float32)
    return lax.fori_loop(begin_slot, end_slot, one_task, start_sum)


def body(amplitudes, integrals, cd_index, live_blocks, occ_energy, vir_energy):
    cycle_size = lax.axis_size("blk")
    here_index = lax.axis_index("blk")
    slot_count = integrals.shape[0]
    own_block = amplitudes[0]
    cycle_reach = REACH
    below_list = []
    above_list = []
    for stride in range(1, cycle_reach + 1):
        below_list.append(shifted(own_block, "blk", stride))
        above_list.append(shifted(own_block, "blk", -stride))
    nearby = jnp.stack(below_list[::-1] + [own_block] + above_list)
    my_live = live_blocks[here_index]
    my_cd = lax.dynamic_slice_in_dim(cd_index, here_index * slot_count, slot_count)
    my_offsets = cycle_offsets(my_cd, here_index, cycle_reach, cycle_size)
    denominator = vir_energy[0][None, :] - occ_energy[:, None]
    ladder = sum_at_owner(contract_tasks(nearby, integrals, my_offsets, 0, my_live), "grp", 0)
    return (ladder / denominator)[None]


def solution(mesh):
    return jax.shard_map(
        body,
        mesh=mesh,
        in_specs=(P("blk", None, "grp"), P("blk", "grp", None), P(), P(), P("grp"), P("blk", None)),
        out_specs=P("blk", "grp", None),
        check_vma=False,
    )
```

profile of v0, /device:TPU:10, one launch (start us, length us, event | category | flops | bytes accessed | tf_op | source)
XLA Modules:
  0.0 100.9 jit_solution(14653849189281736399)
XLA Ops:
  0.0 5.2 %collective-permute-start = (bf16[512,256]{1,0:T(8,128)(2,1)}, bf16[512,256]{1,0:T(8,128)(2,1)S(1)}, u32[]{:S(2)}, u32[]{:S(2)}) collective-permute-start(bf16[512,256]{1,0:T(8,128)(2,1)} %bitcast.28), channel_id=1, source_target_pairs={{0,8},{4,12},{8,16},{12,20},{16,24},{20,28},{24,32},{28,36},{32,40... | collective-permute-start | bytes 786440 | tf_op jit(solution)/shard_map/ppermute | solution.py:12
  5.2 8.5 %collective-permute-start.3 = (bf16[512,256]{1,0:T(8,128)(2,1)}, bf16[512,256]{1,0:T(8,128)(2,1)S(1)}, u32[]{:S(2)}, u32[]{:S(2)}) collective-permute-start(bf16[512,256]{1,0:T(8,128)(2,1)} %bitcast.29), channel_id=1, source_target_pairs={{0,504},{4,508},{8,0},{12,4},{16,8},{20,12},{24,16},{28,20},{32,24... | collective-permute-start | bytes 786440 | tf_op jit(solution)/shard_map/ppermute | solution.py:12
  13.7 4.4 %collective-permute-start.2 = (bf16[512,256]{1,0:T(8,128)(2,1)}, bf16[512,256]{1,0:T(8,128)(2,1)S(1)}, u32[]{:S(2)}, u32[]{:S(2)}) collective-permute-start(bf16[512,256]{1,0:T(8,128)(2,1)} %bitcast.30), channel_id=1, source_target_pairs={{0,508},{4,0},{8,4},{12,8},{16,12},{20,16},{24,20},{28,24},{32,28}... | collective-permute-start | bytes 786440 | tf_op jit(solution)/shard_map/ppermute | solution.py:12
  18.0 1.9 %collective-permute-start.1 = (bf16[512,256]{1,0:T(8,128)(2,1)}, bf16[512,256]{1,0:T(8,128)(2,1)S(1)}, u32[]{:S(2)}, u32[]{:S(2)}) collective-permute-start(bf16[512,256]{1,0:T(8,128)(2,1)} %bitcast.31), channel_id=1, source_target_pairs={{0,4},{4,8},{8,12},{12,16},{16,20},{20,24},{24,28},{28,32},{32,36}... | collective-permute-start | bytes 786440 | tf_op jit(solution)/shard_map/ppermute | solution.py:12
  20.0 0.8 and_select_fusion
  20.8 1.2 %dynamic_slice.15 = s32[1]{0:T(128)} dynamic-slice(s32[128]{0:T(128)} %param.11, s32[]{:T(128)S(6)} %select_n.20), dynamic_slice_sizes={1} | dynamic-slice | bytes 12 | tf_op jit(solution)/shard_map/dynamic_slice | solution.py:55
  22.0 0.0 collective-permute-done
  22.0 7.4 %collective-permute-done.1 = bf16[512,256]{1,0:T(8,128)(2,1)S(1)} collective-permute-done((bf16[512,256]{1,0:T(8,128)(2,1)}, bf16[512,256]{1,0:T(8,128)(2,1)S(1)}, u32[]{:S(2)}, u32[]{:S(2)}) %collective-permute-start.1) | collective-permute-done | bytes 262176 | tf_op jit(solution)/shard_map/ppermute | solution.py:12
  29.5 1.0 constant_dynamic-update-slice_fusion
  30.5 0.3 collective-permute-done.2
  30.8 0.0 collective-permute-done.3
  30.8 0.2 broadcast_in_dim.2
  31.1 36.1 %while.10 = (s32[]{:T(128)}, f32[512,1024]{1,0:T(8,128)S(1)}, s32[]{:T(128)}, s32[8]{0:T(128)S(1)}, bf16[5,512,256]{2,1,0:T(8,128)(2,1)S(1)}, /*index=5*/bf16[8,...) while((s32[]{:T(128)}, f32[512,1024]{1,0:T(8,128)S(1)}, s32[]{:T(128)}, ...), condition=%wide.region_1.2_spmd, body=%wide.region_0.1_spmd.sunk | while | flops 268959744 | bytes 4980933 | solution.py:40
  31.7 0.6 dynamic_slice.31
  34.0 1.5 %convolution_add_fusion.2 = f32[512,1024]{1,0:T(8,128)S(1)} fusion(f32[512,1024]{1,0:T(8,128)S(1)} %get-tuple-element.100, bf16[8,256,1024]{2,1,0:T(8,128)(2,1)} %get-tuple-element.114, s32[]{:T(128)S(6)} %select_n.26, bf16[5,512,256]{2,1,0:T(8,128)(2,1)S(1)} %get-tuple-element.113, s32[]{:T(128)S(6)} %select_n.27), kind=kOutput, calls=%fused_computation.clone.1 | convolution fusion | flops 268959744 | bytes 4980744 | tf_op jit(solution)/shard_map/while/body/dot_general | solution.py:37
  36.1 0.6 dynamic_slice.31
  38.4 1.5 %convolution_add_fusion.2 = f32[512,1024]{1,0:T(8,128)S(1)} fusion(f32[512,1024]{1,0:T(8,128)S(1)} %get-tuple-element.100, bf16[8,256,1024]{2,1,0:T(8,128)(2,1)} %get-tuple-element.114, s32[]{:T(128)S(6)} %select_n.26, bf16[5,512,256]{2,1,0:T(8,128)(2,1)S(1)} %get-tuple-element.113, s32[]{:T(128)S(6)} %select_n.27), kind=kOutput, calls=%fused_computation.clone.1 | convolution fusion | flops 268959744 | bytes 4980744 | tf_op jit(solution)/shard_map/while/body/dot_general | solution.py:37
  40.6 0.6 dynamic_slice.31
  42.8 1.5 %convolution_add_fusion.2 = f32[512,1024]{1,0:T(8,128)S(1)} fusion(f32[512,1024]{1,0:T(8,128)S(1)} %get-tuple-element.100, bf16[8,256,1024]{2,1,0:T(8,128)(2,1)} %get-tuple-element.114, s32[]{:T(128)S(6)} %select_n.26, bf16[5,512,256]{2,1,0:T(8,128)(2,1)S(1)} %get-tuple-element.113, s32[]{:T(128)S(6)} %select_n.27), kind=kOutput, calls=%fused_computation.clone.1 | convolution fusion | flops 268959744 | bytes 4980744 | tf_op jit(solution)/shard_map/while/body/dot_general | solution.py:37
  45.0 0.6 dynamic_slice.31
  47.3 1.5 %convolution_add_fusion.2 = f32[512,1024]{1,0:T(8,128)S(1)} fusion(f32[512,1024]{1,0:T(8,128)S(1)} %get-tuple-element.100, bf16[8,256,1024]{2,1,0:T(8,128)(2,1)} %get-tuple-element.114, s32[]{:T(128)S(6)} %select_n.26, bf16[5,512,256]{2,1,0:T(8,128)(2,1)S(1)} %get-tuple-element.113, s32[]{:T(128)S(6)} %select_n.27), kind=kOutput, calls=%fused_computation.clone.1 | convolution fusion | flops 268959744 | bytes 4980744 | tf_op jit(solution)/shard_map/while/body/dot_general | solution.py:37
  49.4 0.6 dynamic_slice.31
  51.7 1.5 %convolution_add_fusion.2 = f32[512,1024]{1,0:T(8,128)S(1)} fusion(f32[512,1024]{1,0:T(8,128)S(1)} %get-tuple-element.100, bf16[8,256,1024]{2,1,0:T(8,128)(2,1)} %get-tuple-element.114, s32[]{:T(128)S(6)} %select_n.26, bf16[5,512,256]{2,1,0:T(8,128)(2,1)S(1)} %get-tuple-element.113, s32[]{:T(128)S(6)} %select_n.27), kind=kOutput, calls=%fused_computation.clone.1 | convolution fusion | flops 268959744 | bytes 4980744 | tf_op jit(solution)/shard_map/while/body/dot_general | solution.py:37
  53.9 0.6 dynamic_slice.31
  56.1 1.5 %convolution_add_fusion.2 = f32[512,1024]{1,0:T(8,128)S(1)} fusion(f32[512,1024]{1,0:T(8,128)S(1)} %get-tuple-element.100, bf16[8,256,1024]{2,1,0:T(8,128)(2,1)} %get-tuple-element.114, s32[]{:T(128)S(6)} %select_n.26, bf16[5,512,256]{2,1,0:T(8,128)(2,1)S(1)} %get-tuple-element.113, s32[]{:T(128)S(6)} %select_n.27), kind=kOutput, calls=%fused_computation.clone.1 | convolution fusion | flops 268959744 | bytes 4980744 | tf_op jit(solution)/shard_map/while/body/dot_general | solution.py:37
  58.3 0.6 dynamic_slice.31
  60.6 1.5 %convolution_add_fusion.2 = f32[512,1024]{1,0:T(8,128)S(1)} fusion(f32[512,1024]{1,0:T(8,128)S(1)} %get-tuple-element.100, bf16[8,256,1024]{2,1,0:T(8,128)(2,1)} %get-tuple-element.114, s32[]{:T(128)S(6)} %select_n.26, bf16[5,512,256]{2,1,0:T(8,128)(2,1)S(1)} %get-tuple-element.113, s32[]{:T(128)S(6)} %select_n.27), kind=kOutput, calls=%fused_computation.clone.1 | convolution fusion | flops 268959744 | bytes 4980744 | tf_op jit(solution)/shard_map/while/body/dot_general | solution.py:37
  62.7 0.6 dynamic_slice.31
  65.0 1.5 %convolution_add_fusion.2 = f32[512,1024]{1,0:T(8,128)S(1)} fusion(f32[512,1024]{1,0:T(8,128)S(1)} %get-tuple-element.100, bf16[8,256,1024]{2,1,0:T(8,128)(2,1)} %get-tuple-element.114, s32[]{:T(128)S(6)} %select_n.26, bf16[5,512,256]{2,1,0:T(8,128)(2,1)S(1)} %get-tuple-element.113, s32[]{:T(128)S(6)} %select_n.27), kind=kOutput, calls=%fused_computation.clone.1 | convolution fusion | flops 268959744 | bytes 4980744 | tf_op jit(solution)/shard_map/while/body/dot_general | solution.py:37
  67.2 31.0 %all_to_all.5 = f32[4,128,1024]{2,1,0:T(8,128)} all-to-all(f32[4,128,1024]{2,1,0:T(8,128)S(1)} %bitcast.27), channel_id=1, replica_groups=mesh['blk'=128,'grp'=4] {'grp'}, dimensions={0} | all-to-all | bytes 4194304 | tf_op jit(solution)/shard_map/all_to_all | solution.py:23
  98.1 0.0 copy-start
  98.1 0.0 copy-start.1
  98.1 1.8 %reduce_sum.11 = f32[128,1024]{1,0:T(8,128)S(1)} reduce(f32[4,128,1024]{2,1,0:T(8,128)} %all_to_all.5, f32[]{:T(128)} %constant.18.clone.1), dimensions={0}, to_apply=%region_2.3 | reduce | flops 393216 | bytes 2621444 | tf_op jit(solution)/shard_map/reduce_sum | solution.py:24
  99.9 0.0 copy-done
  99.9 0.0 copy-done.1
  100.0 0.9 bitcast_divide_fusion
  (4 shorter events, 0.1 us)
Async XLA Ops:
  0.0 22.0 %collective-permute-start = (bf16[512,256]{1,0:T(8,128)(2,1)}, bf16[512,256]{1,0:T(8,128)(2,1)S(1)}, u32[]{:S(2)}, u32[]{:S(2)}) collective-permute-start(bf16[512,256]{1,0:T(8,128)(2,1)} %bitcast.28), channel_id=1, source_target_pairs={{0,8},{4,12},{8,16},{12,20},{16,24},{20,28},{24,32},{28,36},{32,40... | collective-permute-start | bytes 786440 | tf_op jit(solution)/shard_map/ppermute | solution.py:12
  5.2 25.6 %collective-permute-start.3 = (bf16[512,256]{1,0:T(8,128)(2,1)}, bf16[512,256]{1,0:T(8,128)(2,1)S(1)}, u32[]{:S(2)}, u32[]{:S(2)}) collective-permute-start(bf16[512,256]{1,0:T(8,128)(2,1)} %bitcast.29), channel_id=1, source_target_pairs={{0,504},{4,508},{8,0},{12,4},{16,8},{20,12},{24,16},{28,20},{32,24... | collective-permute-start | bytes 786440 | tf_op jit(solution)/shard_map/ppermute | solution.py:12
  13.7 17.1 %collective-permute-start.2 = (bf16[512,256]{1,0:T(8,128)(2,1)}, bf16[512,256]{1,0:T(8,128)(2,1)S(1)}, u32[]{:S(2)}, u32[]{:S(2)}) collective-permute-start(bf16[512,256]{1,0:T(8,128)(2,1)} %bitcast.30), channel_id=1, source_target_pairs={{0,508},{4,0},{8,4},{12,8},{16,12},{20,16},{24,20},{28,24},{32,28}... | collective-permute-start | bytes 786440 | tf_op jit(solution)/shard_map/ppermute | solution.py:12
  18.0 11.4 %collective-permute-start.1 = (bf16[512,256]{1,0:T(8,128)(2,1)}, bf16[512,256]{1,0:T(8,128)(2,1)S(1)}, u32[]{:S(2)}, u32[]{:S(2)}) collective-permute-start(bf16[512,256]{1,0:T(8,128)(2,1)} %bitcast.31), channel_id=1, source_target_pairs={{0,4},{4,8},{8,12},{12,16},{16,20},{20,24},{24,28},{28,32},{32,36}... | collective-permute-start | bytes 786440 | tf_op jit(solution)/shard_map/ppermute | solution.py:12
  98.1 1.8 %copy-start = (f32[1,1024]{1,0:T(1,128)S(1)}, f32[1,1024]{1,0:T(1,128)}, u32[]{:S(2)}) copy-start(f32[1,1024]{1,0:T(1,128)} %param.13) | copy-start | bytes 12292
  98.1 1.8 %copy-start.1 = (f32[128]{0:T(128)S(1)}, f32[128]{0:T(128)}, u32[]{:S(2)}) copy-start(f32[128]{0:T(128)} %param.12) | copy-start | bytes 1540
where the time goes:
time: 102 us; the launch traced here: 101 us
  blocking collectives  31 us (30%)
  starting transfers between devices  19.9 us (20%)
  loops' own time  19.2 us (19%)
  matrix products  12.2 us (12%)
  waiting for transfers between devices  7.74 us (8%)
  local copies, waits for them, and re-layouts  7.18 us (7%)
  other arithmetic  3.51 us (3%)
    all_to_all x1, blocking collectives, sum_at_owner(): lax.all_to_all(tiles, axis, split_axis=0, concat_axis=0, tiled=True)  31 us
    ppermute x4, starting transfers between devices, shifted(): return lax.ppermute(value, axis, pairs)  19.9 us
    another operation x1, loops' own time, contract_tasks(): return lax.fori_loop(begin_slot, end_slot, one_task, start_sum)  19.2 us
    dot_general x8, matrix products, one_task(): jnp.dot(amp_block, pieces[slot_index], preferred_element_type=jnp.float32)  12.2 us
    ppermute x4, waiting for transfers between devices, shifted(): return lax.ppermute(value, axis, pairs)  7.74 us
    dynamic_slice x8, local copies, waits for them, and re-layouts, one_task(): amp_block = nearby[offsets[slot_index]]  4.64 us
  transfers between devices with their start and end apart: 4, of which 2 were waited for; matrix products, arithmetic and copies ran while one was open for 3% of the time, Pallas kernels for 0%

commit v1 on v0

v1 whole, which is shorter than its diff:
```python
import functools

import jax
import jax.numpy as jnp
from jax import lax
from jax.experimental import pallas as pl
from jax.experimental.pallas import tpu as pltpu
from jax.sharding import PartitionSpec as P

REACH = 2
LEVELS = 32767.0
LOG_STEPS = 128.0
LEAST_PEAK = 2.0**-120
VMEM_BYTES = 48 * 1024 * 1024

VMEM = pl.BlockSpec(memory_space=pltpu.VMEM)
SMEM = pl.BlockSpec(memory_space=pltpu.SMEM)


def shifted(value, axis, steps):
    count = lax.axis_size(axis)
    pairs = [(source, (source + steps) % count) for source in range(count)]
    return lax.ppermute(value, axis, pairs)


def rows_of(block, height):
    return pl.ds(pl.multiple_of(block * height, height), height)


def row_order(grp):
    high, core = grp // 2, lax.rem(grp, 2)
    return [2 * h + c for c in (core, 1 - core) for h in (high, 1 - high)]


def ladder_kernel(place_ref, cd_ref, live_ref, *refs):
    blocks, (integrals_ref, keep_ref, send_ref, near_ref) = refs[: 2 * REACH + 1], refs[2 * REACH + 1 :]
    here, grp = place_ref[0], place_ref[1]
    slots, depth, width = integrals_ref.shape
    height = keep_ref.shape[0] // 2
    cycle = live_ref.shape[0]
    for at, block in enumerate(row_order(grp)):
        for offset, source in enumerate(blocks):
            near_ref[offset, at * height : (at + 1) * height, :] = source[rows_of(block, height), :]
    keep_ref[...] = jnp.zeros_like(keep_ref)
    send_ref[...] = jnp.zeros_like(send_ref)

    def one_slot(slot, carry):
        offset = lax.rem(cd_ref[here * slots + slot] - here + (REACH + cycle), cycle)
        for half, target in enumerate((keep_ref, send_ref)):
            amp = near_ref[offset, 2 * half * height : 2 * (half + 1) * height, :]
            for column in range(0, width, 256):
                target[:, column : column + 256] += jnp.dot(
                    amp, integrals_ref[slot, :, column : column + 256], preferred_element_type=jnp.float32
                )
        return carry

    lax.fori_loop(0, live_ref[here], one_slot, 0)


def encode_kernel(keep_ref, arrived_ref, code_ref):
    height, width = keep_ref.shape[0] // 2, keep_ref.shape[1]
    marks = []
    for chunk in range(width // 128):
        columns = slice(chunk * 128, (chunk + 1) * 128)
        value = keep_ref[height:, columns] + arrived_ref[height:, columns]
        peak = jnp.maximum(jnp.max(jnp.abs(value), axis=0, keepdims=True), LEAST_PEAK)
        mark = jnp.ceil(jnp.log2(peak) * LOG_STEPS)
        marks.append(mark)
        level = jnp.clip(jnp.round(value * jnp.exp2(mark * (-1.0 / LOG_STEPS)) * LEVELS), -LEVELS, LEVELS)
        code_ref[chunk * height : (chunk + 1) * height, :] = level.astype(jnp.int32).astype(jnp.int16)
    tail = jnp.concatenate(marks + [jnp.zeros_like(marks[0])] * (16 - len(marks)), axis=0)
    code_ref[len(marks) * height :, :] = tail.astype(jnp.int32).astype(jnp.int16)


def finish_kernel(keep_ref, arrived_ref, code_ref, occ_ref, vir_ref, out_ref):
    height, width = out_ref.shape
    chunks = width // 128
    marks = code_ref[chunks * height :, :].astype(jnp.int32).astype(jnp.float32)
    scales = jnp.exp2(marks * (1.0 / LOG_STEPS)) * (1.0 / LEVELS)
    for chunk in range(chunks):
        columns = slice(chunk * 128, (chunk + 1) * 128)
        other = code_ref[chunk * height : (chunk + 1) * height, :].astype(jnp.int32).astype(jnp.float32)
        total = keep_ref[:height, columns] + arrived_ref[:height, columns] + other * scales[chunk : chunk + 1, :]
        out_ref[:, columns] = total / (vir_ref[:, columns] - occ_ref[...])


def call(kernel, out_shape, specs, scratch=(), flops=0):
    return pl.pallas_call(
        kernel,
        out_shape=out_shape,
        in_specs=specs,
        out_specs=jax.tree.map(lambda _: VMEM, out_shape),
        scratch_shapes=scratch,
        compiler_params=pltpu.CompilerParams(vmem_limit_bytes=VMEM_BYTES),
        cost_estimate=pl.CostEstimate(flops=flops, bytes_accessed=4 << 20, transcendentals=0),
    )


def body(amplitudes, integrals, cd_index, live_blocks, occ_energy, vir_energy):
    own = amplitudes[0]
    rows, depth = own.shape
    slots, _, width = integrals.shape
    height = rows // lax.axis_size("grp")
    arrived = {step: shifted(own, "blk", -step) for step in (2, -2, 1, -1)}
    blocks = [arrived[step] if step else own for step in range(-REACH, REACH + 1)]
    place = jnp.stack([lax.axis_index("blk"), lax.axis_index("grp")]).astype(jnp.int32)
    half = jax.ShapeDtypeStruct((2 * height, width), jnp.float32)
    keep, send = call(
        ladder_kernel,
        (half, half),
        [SMEM] * 3 + [VMEM] * (len(blocks) + 1),
        [pltpu.VMEM((len(blocks), rows, depth), own.dtype)],
        2 * slots * rows * depth * width,
    )(place, cd_index, live_blocks, *blocks, integrals)
    other_core = lax.ppermute(send, "grp", [(0, 1), (1, 0), (2, 3), (3, 2)])
    chunks = width // 128
    code = call(encode_kernel, jax.ShapeDtypeStruct((chunks * height + 16, 128), jnp.int16), [VMEM] * 2)(keep, other_core)
    other_chip = lax.ppermute(code, "grp", [(0, 2), (1, 3), (2, 0), (3, 1)])
    out = call(finish_kernel, jax.ShapeDtypeStruct((height, width), jnp.float32), [VMEM] * 5)(
        keep, other_core, other_chip, occ_energy[:, None], vir_energy
    )
    return out[None]


def solution(mesh):
    return jax.shard_map(
        body,
        mesh=mesh,
        in_specs=(P("blk", None, "grp"), P("blk", "grp", None), P(), P(), P("grp"), P("blk", None)),
        out_specs=P("blk", "grp", None),
        check_vma=False,
    )
```

time: 102 us -> 60.7 us (0.60)
  the two profiles are of different devices: /device:TPU:10 before, /device:TPU:1 now
where the time goes in v1:
time: 60.7 us; the launch traced here: 60.4 us
  starting transfers between devices  32.6 us (54%)
  waiting for transfers between devices  19.4 us (32%)
  Pallas kernels  5.79 us (10%)
  local copies, waits for them, and re-layouts  2.41 us (4%)
    ppermute x4, starting transfers between devices, shifted(): return lax.ppermute(value, axis, pairs)  23.3 us
    ppermute x4, waiting for transfers between devices, shifted(): return lax.ppermute(value, axis, pairs)  10.8 us
    ppermute x1, waiting for transfers between devices, body(): other_chip = lax.ppermute(code, 'grp', [(0, 2), (1, 3), (2, 0), (3, 1)])  6.35 us
    ppermute x1, starting transfers between devices, body(): other_core = lax.ppermute(send, 'grp', [(0, 1), (1, 0), (2, 3), (3, 2)])  4.83 us
    pallas_call x1, Pallas kernels, body(): call(ladder_kernel, (half, half), [SMEM] * 3 + [VMEM] * (len(blocks) + 1)...  4.62 us
    ppermute x1, starting transfers between devices, body(): other_chip = lax.ppermute(code, 'grp', [(0, 2), (1, 3), (2, 0), (3, 1)])  4.53 us
    unnamed x10, local copies, waits for them, and re-layouts  2.3 us
    ppermute x1, waiting for transfers between devices, body(): other_core = lax.ppermute(send, 'grp', [(0, 1), (1, 0), (2, 3), (3, 2)])  2.26 us
  transfers between devices with their start and end apart: 6, of which 4 were waited for; matrix products, arithmetic and copies ran while one was open for 0% of the time, Pallas kernels for 0%

profile of v1, /device:TPU:1, one launch (start us, length us, event | category | flops | bytes accessed | tf_op | source)
XLA Modules:
  0.0 60.4 jit_solution(5742325397734722714)
XLA Ops:
  0.0 5.7 %collective-permute-start = (bf16[512,256]{1,0:T(8,128)(2,1)}, bf16[512,256]{1,0:T(8,128)(2,1)S(1)}, u32[]{:S(2)}, u32[]{:S(2)}) collective-permute-start(bf16[512,256]{1,0:T(8,128)(2,1)} %bitcast.5), channel_id=1, source_target_pairs={{0,8},{4,12},{8,16},{12,20},{16,24},{20,28},{24,32},{28,36},{32,40... | collective-permute-start | bytes 786440 | tf_op jit(solution)/shard_map/ppermute | solution.py:23
  5.7 3.5 %collective-permute-start.1 = (bf16[512,256]{1,0:T(8,128)(2,1)}, bf16[512,256]{1,0:T(8,128)(2,1)S(1)}, u32[]{:S(2)}, u32[]{:S(2)}) collective-permute-start(bf16[512,256]{1,0:T(8,128)(2,1)} %bitcast.6), channel_id=1, source_target_pairs={{0,4},{4,8},{8,12},{12,16},{16,20},{20,24},{24,28},{28,32},{32,36}... | collective-permute-start | bytes 786440 | tf_op jit(solution)/shard_map/ppermute | solution.py:23
  9.3 9.7 %collective-permute-start.2 = (bf16[512,256]{1,0:T(8,128)(2,1)}, bf16[512,256]{1,0:T(8,128)(2,1)S(1)}, u32[]{:S(2)}, u32[]{:S(2)}) collective-permute-start(bf16[512,256]{1,0:T(8,128)(2,1)} %bitcast.7), channel_id=1, source_target_pairs={{0,508},{4,0},{8,4},{12,8},{16,12},{20,16},{24,20},{28,24},{32,28}... | collective-permute-start | bytes 786440 | tf_op jit(solution)/shard_map/ppermute | solution.py:23
  19.0 4.3 %collective-permute-start.3 = (bf16[512,256]{1,0:T(8,128)(2,1)}, bf16[512,256]{1,0:T(8,128)(2,1)S(1)}, u32[]{:S(2)}, u32[]{:S(2)}) collective-permute-start(bf16[512,256]{1,0:T(8,128)(2,1)} %bitcast.8), channel_id=1, source_target_pairs={{0,504},{4,508},{8,0},{12,4},{16,8},{20,12},{24,16},{28,20},{32,24... | collective-permute-start | bytes 786440 | tf_op jit(solution)/shard_map/ppermute | solution.py:23
  23.3 0.0 copy-start.4
  23.3 0.1 pad_add_fusion.place_ref
  23.4 0.0 copy-start
  23.4 0.0 collective-permute-done.refs_0_
  23.4 9.5 %collective-permute-done.1.refs_1_ = bf16[512,256]{1,0:T(8,128)(2,1)S(1)} collective-permute-done((bf16[512,256]{1,0:T(8,128)(2,1)}, bf16[512,256]{1,0:T(8,128)(2,1)S(1)}, u32[]{:S(2)}, u32[]{:S(2)}) %collective-permute-start.1) | collective-permute-done | bytes 262176 | tf_op jit(solution)/shard_map/ppermute | solution.py:23
  32.9 0.0 collective-permute-done.2.refs_3_
  32.9 1.2 %collective-permute-done.3.refs_4_ = bf16[512,256]{1,0:T(8,128)(2,1)S(1)} collective-permute-done((bf16[512,256]{1,0:T(8,128)(2,1)}, bf16[512,256]{1,0:T(8,128)(2,1)S(1)}, u32[]{:S(2)}, u32[]{:S(2)}) %collective-permute-start.3) | collective-permute-done | bytes 262176 | tf_op jit(solution)/shard_map/ppermute | solution.py:23
  34.2 0.0 copy-start.1
  34.2 0.9 %copy-done.1 = bf16[1,512,256]{2,1,0:T(8,128)(2,1)S(1)} copy-done((bf16[1,512,256]{2,1,0:T(8,128)(2,1)S(1)}, bf16[1,512,256]{2,1,0:T(8,128)(2,1)}, u32[]{:S(2)}) %copy-start.1) | copy-done | bytes 262168
  35.1 0.0 copy-start.2
  35.1 0.7 %copy-done.2 = s32[1024]{0:T(1024)S(1)} copy-done((s32[1024]{0:T(1024)S(1)}, s32[1024]{0:T(1024)}, u32[]{:S(2)}) %copy-start.2) | copy-done | bytes 4120
  35.8 0.0 copy-start.3
  35.8 0.7 %copy-done.3 = s32[128]{0:T(128)S(1)} copy-done((s32[128]{0:T(128)S(1)}, s32[128]{0:T(128)}, u32[]{:S(2)}) %copy-start.3) | copy-done | bytes 536
  36.4 4.6 %shard_map.64 = (f32[256,1024]{1,0:T(8,128)S(1)}, f32[256,1024]{1,0:T(8,128)S(1)}) custom-call(s32[2]{0:T(128)S(1)} %pad_add_fusion.place_ref, s32[1024]{0:T(1024)S(1)} %copy-done.2, s32[128]{0:T(128)S(1)} %copy-done.3, bf16[512,256]{1,0:T(8,128)(2,1)S(1)} %collective-permute-done.refs_0_, bf16[512,256]{1,0:T(8,128)(2,1)S(1)} %collective-permute-done.1.refs_1_, ...), custom_call_target="tpu_custom_call" | custom-call | flops 2147483648 | bytes 4194304 | tf_op jit(solution)/shard_map/pallas_call | solution.py:108
  41.1 4.8 %collective-permute-start.4 = (f32[256,1024]{1,0:T(8,128)S(1)}, f32[256,1024]{1,0:T(8,128)S(1)}, u32[]{:S(2)}, u32[]{:S(2)}) collective-permute-start(f32[256,1024]{1,0:T(8,128)S(1)} %get-tuple-element.8), channel_id=1, source_target_pairs={{0,1},{1,0},{2,3},{3,2},{4,5},{5,4},{6,7},{7,6},{8,9},{9,8},{10,11... | collective-permute-start | bytes 3145736 | tf_op jit(solution)/shard_map/ppermute | solution.py:115
  45.9 2.3 %collective-permute-done.4.arrived_ref = f32[256,1024]{1,0:T(8,128)S(1)} collective-permute-done((f32[256,1024]{1,0:T(8,128)S(1)}, f32[256,1024]{1,0:T(8,128)S(1)}, u32[]{:S(2)}, u32[]{:S(2)}) %collective-permute-start.4) | collective-permute-done | bytes 1048608 | tf_op jit(solution)/shard_map/ppermute | solution.py:115
  48.2 0.2 shard_map.65
  48.3 4.5 %collective-permute-start.5 = (s16[1040,128]{1,0:T(8,128)(2,1)S(1)}, s16[1040,128]{1,0:T(8,128)(2,1)S(1)}, u32[]{:S(2)}, u32[]{:S(2)}) collective-permute-start(s16[1040,128]{1,0:T(8,128)(2,1)S(1)} %shard_map.65), channel_id=1, source_target_pairs={{0,2},{1,3},{2,0},{3,1},{4,6},{5,7},{6,4},{7,5},{8,10},{9,11},{10,... | collective-permute-start | bytes 798728 | tf_op jit(solution)/shard_map/ppermute | solution.py:118
  52.9 0.0 copy-done.4
  52.9 0.1 copy.7.occ_ref
  53.0 6.3 %collective-permute-done.5.code_ref = s16[1040,128]{1,0:T(8,128)(2,1)S(1)} collective-permute-done((s16[1040,128]{1,0:T(8,128)(2,1)S(1)}, s16[1040,128]{1,0:T(8,128)(2,1)S(1)}, u32[]{:S(2)}, u32[]{:S(2)}) %collective-permute-start.5) | collective-permute-done | bytes 266272 | tf_op jit(solution)/shard_map/ppermute | solution.py:118
  59.3 0.0 copy-done
  59.4 1.0 %shard_map.66 = f32[128,1024]{1,0:T(8,128)} custom-call(f32[256,1024]{1,0:T(8,128)S(1)} %get-tuple-element.7.keep_ref, f32[256,1024]{1,0:T(8,128)S(1)} %collective-permute-done.4.arrived_ref, s16[1040,128]{1,0:T(8,128)(2,1)S(1)} %collective-permute-done.5.code_ref, f32[128,1]{1,0:T(8,128)S(1)} %copy.7.occ_ref, f32[1,1024]{1,0:T(1,128)S(1)} %copy-done), custom_call_target="tpu_custom_call" | custom-call | bytes 4194304 | tf_op jit(solution)/shard_map/pallas_call | solution.py:119
Async XLA Ops:
  0.0 23.4 %collective-permute-start = (bf16[512,256]{1,0:T(8,128)(2,1)}, bf16[512,256]{1,0:T(8,128)(2,1)S(1)}, u32[]{:S(2)}, u32[]{:S(2)}) collective-permute-start(bf16[512,256]{1,0:T(8,128)(2,1)} %bitcast.5), channel_id=1, source_target_pairs={{0,8},{4,12},{8,16},{12,20},{16,24},{20,28},{24,32},{28,36},{32,40... | collective-permute-start | bytes 786440 | tf_op jit(solution)/shard_map/ppermute | solution.py:23
  5.7 27.2 %collective-permute-start.1 = (bf16[512,256]{1,0:T(8,128)(2,1)}, bf16[512,256]{1,0:T(8,128)(2,1)S(1)}, u32[]{:S(2)}, u32[]{:S(2)}) collective-permute-start(bf16[512,256]{1,0:T(8,128)(2,1)} %bitcast.6), channel_id=1, source_target_pairs={{0,4},{4,8},{8,12},{12,16},{16,20},{20,24},{24,28},{28,32},{32,36}... | collective-permute-start | bytes 786440 | tf_op jit(solution)/shard_map/ppermute | solution.py:23
  9.3 23.7 %collective-permute-start.2 = (bf16[512,256]{1,0:T(8,128)(2,1)}, bf16[512,256]{1,0:T(8,128)(2,1)S(1)}, u32[]{:S(2)}, u32[]{:S(2)}) collective-permute-start(bf16[512,256]{1,0:T(8,128)(2,1)} %bitcast.7), channel_id=1, source_target_pairs={{0,508},{4,0},{8,4},{12,8},{16,12},{20,16},{24,20},{28,24},{32,28}... | collective-permute-start | bytes 786440 | tf_op jit(solution)/shard_map/ppermute | solution.py:23
  19.0 15.1 %collective-permute-start.3 = (bf16[512,256]{1,0:T(8,128)(2,1)}, bf16[512,256]{1,0:T(8,128)(2,1)S(1)}, u32[]{:S(2)}, u32[]{:S(2)}) collective-permute-start(bf16[512,256]{1,0:T(8,128)(2,1)} %bitcast.8), channel_id=1, source_target_pairs={{0,504},{4,508},{8,0},{12,4},{16,8},{20,12},{24,16},{28,20},{32,24... | collective-permute-start | bytes 786440 | tf_op jit(solution)/shard_map/ppermute | solution.py:23
  23.3 29.6 %copy-start.4 = (f32[128]{0:T(128)S(1)}, f32[128]{0:T(128)}, u32[]{:S(2)}) copy-start(f32[128]{0:T(128)} %param.10) | copy-start | bytes 1540
  23.4 36.0 %copy-start = (f32[1,1024]{1,0:T(1,128)S(1)}, f32[1,1024]{1,0:T(1,128)}, u32[]{:S(2)}) copy-start(f32[1,1024]{1,0:T(1,128)} %vir_ref.1) | copy-start | bytes 12292
  34.2 0.9 %copy-start.1 = (bf16[1,512,256]{2,1,0:T(8,128)(2,1)S(1)}, bf16[1,512,256]{2,1,0:T(8,128)(2,1)}, u32[]{:S(2)}) copy-start(bf16[1,512,256]{2,1,0:T(8,128)(2,1)} %param.6) | copy-start | bytes 786436
  35.1 0.7 %copy-start.2 = (s32[1024]{0:T(1024)S(1)}, s32[1024]{0:T(1024)}, u32[]{:S(2)}) copy-start(s32[1024]{0:T(1024)} %cd_ref.1) | copy-start | bytes 12292
  35.8 0.7 %copy-start.3 = (s32[128]{0:T(128)S(1)}, s32[128]{0:T(128)}, u32[]{:S(2)}) copy-start(s32[128]{0:T(128)} %live_ref.1) | copy-start | bytes 1540
  41.1 7.1 %collective-permute-start.4 = (f32[256,1024]{1,0:T(8,128)S(1)}, f32[256,1024]{1,0:T(8,128)S(1)}, u32[]{:S(2)}, u32[]{:S(2)}) collective-permute-start(f32[256,1024]{1,0:T(8,128)S(1)} %get-tuple-element.8), channel_id=1, source_target_pairs={{0,1},{1,0},{2,3},{3,2},{4,5},{5,4},{6,7},{7,6},{8,9},{9,8},{10,11... | collective-permute-start | bytes 3145736 | tf_op jit(solution)/shard_map/ppermute | solution.py:115
  48.3 11.0 %collective-permute-start.5 = (s16[1040,128]{1,0:T(8,128)(2,1)S(1)}, s16[1040,128]{1,0:T(8,128)(2,1)S(1)}, u32[]{:S(2)}, u32[]{:S(2)}) collective-permute-start(s16[1040,128]{1,0:T(8,128)(2,1)S(1)} %shard_map.65), channel_id=1, source_target_pairs={{0,2},{1,3},{2,0},{3,1},{4,6},{5,7},{6,4},{7,5},{8,10},{9,11},{10,... | collective-permute-start | bytes 798728 | tf_op jit(solution)/shard_map/ppermute | solution.py:118

commit v2 on v1

v2 whole, which is shorter than its diff:
```python
import jax
import jax.numpy as jnp
from jax import lax
from jax.experimental import pallas as pl
from jax.experimental.pallas import tpu as pltpu
from jax.sharding import PartitionSpec as P

REACH = 2
LEVELS = 32767.0
LOG_STEPS = 128.0
LEAST_PEAK = 2.0**-120
VMEM_BYTES = 32 * 1024 * 1024

VMEM = pl.BlockSpec(memory_space=pltpu.VMEM)
SMEM = pl.BlockSpec(memory_space=pltpu.SMEM)
ANY = pl.BlockSpec(memory_space=pl.ANY)
HBM = pl.BlockSpec(memory_space=pltpu.HBM)


def shifted(value, axis, steps):
    count = lax.axis_size(axis)
    pairs = [(source, (source + steps) % count) for source in range(count)]
    return lax.ppermute(value, axis, pairs)


def call(kernel, out_shape, in_specs, out_specs, scratch=(), flops=0, moved=0, aliases={}):
    return pl.pallas_call(
        kernel,
        out_shape=out_shape,
        in_specs=in_specs,
        out_specs=out_specs,
        scratch_shapes=scratch,
        input_output_aliases=aliases,
        compiler_params=pltpu.CompilerParams(vmem_limit_bytes=VMEM_BYTES),
        cost_estimate=pl.CostEstimate(flops=flops, bytes_accessed=moved, transcendentals=0),
    )


def fetch_kernel(cd_hbm, live_hbm, own_hbm, integrals_hbm, plan_ref, own_ref, integrals_ref, cd_ref, live_ref, sems):
    pairs = [(cd_hbm, cd_ref), (live_hbm, live_ref), (own_hbm, own_ref), (integrals_hbm, integrals_ref)]
    copies = [pltpu.make_async_copy(source, target, sems.at[at]) for at, (source, target) in enumerate(pairs)]
    for copy in copies:
        copy.start()
    copies[0].wait()
    copies[1].wait()
    here, grp = lax.axis_index("blk"), lax.axis_index("grp")
    slots, cycle = integrals_ref.shape[0], live_ref.shape[0]
    for slot in range(slots):
        offset = lax.rem(cd_ref[here * slots + slot] - here + (REACH + cycle), cycle)
        plan_ref[slot] = jnp.where(slot < live_ref[here], offset, -1)
    plan_ref[slots] = grp // 2
    plan_ref[slots + 1] = lax.rem(grp, 2)
    copies[2].wait()
    copies[3].wait()


def gated(value, token):
    return call(
        lambda value_ref, token_ref, out_ref: None,
        jax.ShapeDtypeStruct(value.shape, value.dtype),
        [ANY, ANY],
        ANY,
        aliases={0: 0},
    )(value, token)


def ladder_kernel(among, flips, pieces, plan_ref, integrals_ref, *refs):
    count = len(among) * pieces
    sources, rest = refs[:count], refs[count:]
    out_count = len(flips)
    near_ref = rest[-1]
    outs = rest[-1 - out_count : -1]
    starts = rest[: len(rest) - 1 - out_count]
    slots, depth, width = integrals_ref.shape
    height = outs[0].shape[0] // 2
    high, core = plan_ref[slots], plan_ref[slots + 1]
    for which, group in enumerate(flips):
        for at, (flip_high, flip_core) in enumerate(group):
            block_high = 1 - high if flip_high else high
            block_core = 1 - core if flip_core else core
            target = slice((2 * which + at) * height, (2 * which + at + 1) * height)
            for index in range(len(among)):
                if pieces == 1:
                    rows = pl.ds(pl.multiple_of((2 * block_high + block_core) * height, height), height)
                    near_ref[index, target, :] = sources[index][rows, :]
                else:
                    rows = pl.ds(pl.multiple_of(block_core * height, height), height)
                    for piece in range(2):

                        @pl.when(block_high == piece)
                        def _():
                            near_ref[index, target, :] = sources[2 * index + piece][rows, :]

    for which, out in enumerate(outs):
        out[...] = starts[which][...] if starts else jnp.zeros_like(out)

    def one_slot(slot, carry):
        offset = plan_ref[slot]
        index, wanted = jnp.int32(0), offset == among[0]
        for at in range(1, len(among)):
            index = jnp.where(offset == among[at], at, index)
            wanted = wanted | (offset == among[at])

        @pl.when(wanted)
        def _():
            for column in range(0, width, 256):
                matrix = integrals_ref[slot, :, column : column + 256]
                for which, out in enumerate(outs):
                    amp = near_ref[index, 2 * which * height : 2 * (which + 1) * height, :]
                    out[:, column : column + 256] += jnp.dot(amp, matrix, preferred_element_type=jnp.float32)

        return carry

    lax.fori_loop(0, slots, one_slot, 0)


SEND = ((True, True), (False, True))
MINE = ((True, False), (False, False))


def ladder(among, flips, plan, integrals, blocks, starts=(), after=()):
    slots, depth, width = integrals.shape
    pieces = len(blocks) // len(among)
    height = blocks[0].shape[0] * pieces // 4
    row_count = 2 * height * len(flips)
    out = (jax.ShapeDtypeStruct((2 * height, width), jnp.float32),) * len(flips)
    return call(
        lambda *refs: ladder_kernel(among, flips, pieces, *(refs[: len(refs) - 1 - len(flips) - len(after)] + refs[len(refs) - 1 - len(flips) :])),
        out,
        [SMEM] + [VMEM] * (1 + len(blocks) + len(starts)) + [ANY] * len(after),
        (VMEM,) * len(flips),
        [pltpu.VMEM((len(among), row_count, depth), blocks[0].dtype)],
        2 * 3 * row_count * depth * width,
    )(plan, integrals, *blocks, *starts, *after)


def encode_kernel(mine_ref, arrived_ref, code_ref):
    height, width = mine_ref.shape[0] // 2, mine_ref.shape[1]
    marks = []
    for chunk in range(width // 128):
        columns = slice(chunk * 128, (chunk + 1) * 128)
        value = mine_ref[:height, columns] + arrived_ref[:height, columns]
        peak = jnp.maximum(jnp.max(jnp.abs(value), axis=0, keepdims=True), LEAST_PEAK)
        mark = jnp.ceil(jnp.log2(peak) * LOG_STEPS)
        marks.append(mark)
        level = jnp.clip(jnp.round(value * jnp.exp2(mark * (-1.0 / LOG_STEPS)) * LEVELS), -LEVELS, LEVELS)
        code_ref[chunk * height : (chunk + 1) * height, :] = level.astype(jnp.int32).astype(jnp.int16)
    tail = jnp.concatenate(marks + [jnp.zeros_like(marks[0])] * (16 - len(marks)), axis=0)
    code_ref[len(marks) * height :, :] = tail.astype(jnp.int32).astype(jnp.int16)


def finish_kernel(mine_ref, arrived_ref, code_ref, occ_ref, vir_ref, out_ref):
    height, width = out_ref.shape
    chunks = width // 128
    marks = code_ref[chunks * height :, :].astype(jnp.int32).astype(jnp.float32)
    scales = jnp.exp2(marks * (1.0 / LOG_STEPS)) * (1.0 / LEVELS)
    for chunk in range(chunks):
        columns = slice(chunk * 128, (chunk + 1) * 128)
        other = code_ref[chunk * height : (chunk + 1) * height, :].astype(jnp.int32).astype(jnp.float32)
        total = mine_ref[height:, columns] + arrived_ref[height:, columns] + other * scales[chunk : chunk + 1, :]
        out_ref[:, columns] = total / (vir_ref[:, columns] - occ_ref[...])


def to_other_core(value):
    return lax.ppermute(value, "grp", [(0, 1), (1, 0), (2, 3), (3, 2)])


def to_other_chip(value):
    return lax.ppermute(value, "grp", [(0, 2), (1, 3), (2, 0), (3, 1)])


def body(amplitudes, integrals, cd_index, live_blocks, occ_energy, vir_energy):
    own = amplitudes[0]
    height = own.shape[0] // lax.axis_size("grp")
    slots, depth, width = integrals.shape
    arrived = {step: shifted(own, "blk", -step) for step in (1, -1)}
    plan, own_here, integrals_here = call(
        fetch_kernel,
        (
            jax.ShapeDtypeStruct((slots + 2,), jnp.int32),
            jax.ShapeDtypeStruct(own.shape, own.dtype),
            jax.ShapeDtypeStruct(integrals.shape, integrals.dtype),
        ),
        [HBM] * 4,
        (SMEM, VMEM, VMEM),
        [pltpu.SMEM(cd_index.shape, jnp.int32), pltpu.SMEM(live_blocks.shape, jnp.int32), pltpu.SemaphoreType.DMA((4,))],
        0,
        integrals.size * 2,
    )(*[pltpu.with_memory_space_constraint(x, pltpu.HBM) for x in (cd_index, live_blocks, own, integrals)])
    arrived[1] = gated(arrived[1], plan)
    arrived[-1] = gated(arrived[-1], plan)
    arrived[-2] = shifted(arrived[-1], "blk", 1)
    arrived[2] = shifted(arrived[1], "blk", -1)
    blocks = [arrived[step] if step else own_here for step in range(-REACH, REACH + 1)]
    first_send, first_mine = ladder((1, 3, 2), (SEND, MINE), plan, integrals_here, [blocks[at] for at in (1, 3, 2)])
    (send,) = ladder((0, 4), (SEND,), plan, integrals_here, [blocks[at] for at in (0, 4)], (first_send,))
    arrived_core = to_other_core(send)
    (mine,) = ladder((0, 4), (MINE,), plan, integrals_here, [blocks[at] for at in (0, 4)], (first_mine,), (send,))
    chunks = width // 128
    code = call(
        encode_kernel, jax.ShapeDtypeStruct((chunks * height + 16, 128), jnp.int16), [VMEM] * 2, VMEM, (), 0, 1 << 20
    )(mine, arrived_core)
    code_arrived = to_other_chip(code)
    out = call(
        finish_kernel, jax.ShapeDtypeStruct((height, width), jnp.float32), [VMEM] * 5, VMEM, (), 0, 1 << 20
    )(mine, arrived_core, code_arrived, occ_energy[:, None], vir_energy)
    return out[None]


def solution(mesh):
    return jax.shard_map(
        body,
        mesh=mesh,
        in_specs=(P("blk", None, "grp"), P("blk", "grp", None), P(), P(), P("grp"), P("blk", None)),
        out_specs=P("blk", "grp", None),
        check_vma=False,
    )
```

time: 60.7 us -> 55.7 us (0.918)
  waiting for transfers between devices: 19.4 us -> 10.6 us
  Pallas kernels: 5.79 us -> 9.11 us
  starting transfers between devices: 32.6 us -> 35.4 us
  local copies, waits for them, and re-layouts: 2.41 us -> 0.13 us
    ppermute x4, waiting for transfers between devices: 10.8 us -> 3.7 us  [shifted(): return lax.ppermute(value, axis, pairs)]
    pallas_call x1 -> x6, Pallas kernels: 4.62 us -> 7.94 us  [the longest x3 5.03 us: ladder(): call(lambda *refs: ladder_kernel(among, flips, pieces, *refs[:len(refs) -...]
    ppermute x4, starting transfers between devices: 23.3 us -> 26.6 us  [shifted(): return lax.ppermute(value, axis, pairs)]
    unnamed x10 -> x4, local copies, waits for them, and re-layouts: 2.3 us -> 0.01 us
    ppermute x2, waiting for transfers between devices: 8.61 us -> 6.94 us  [the longest x1 6.35 us: to_other_chip(): return lax.ppermute(value, 'grp', [(0, 2), (1, 3), (2, 0), (3, 1)])]
  transfers between devices with their start and end apart: 6 -> 6, of which waited for: 4 -> 5; matrix products, arithmetic and copies ran while one was open for 0% -> 0% of each run, Pallas kernels for 0% -> 11%
where the time goes in v2:
time: 55.7 us; the launch traced here: 55.4 us
  starting transfers between devices  35.4 us (64%)
  waiting for transfers between devices  10.6 us (19%)
  Pallas kernels  9.11 us (16%)
    ppermute x4, starting transfers between devices, shifted(): return lax.ppermute(value, axis, pairs)  26.6 us
    ppermute x1, waiting for transfers between devices, to_other_chip(): return lax.ppermute(value, 'grp', [(0, 2), (1, 3), (2, 0), (3, 1)])  6.35 us
    pallas_call x3, Pallas kernels, ladder(): call(lambda *refs: ladder_kernel(among, flips, pieces, *refs[:len(refs) -...  5.03 us
    ppermute x1, starting transfers between devices, to_other_chip(): return lax.ppermute(value, 'grp', [(0, 2), (1, 3), (2, 0), (3, 1)])  4.53 us
    ppermute x1, starting transfers between devices, to_other_core(): return lax.ppermute(value, 'grp', [(0, 1), (1, 0), (2, 3), (3, 2)])  4.34 us
    ppermute x4, waiting for transfers between devices, shifted(): return lax.ppermute(value, axis, pairs)  3.7 us
    pallas_call x1, Pallas kernels, body(): call(fetch_kernel, (jax.ShapeDtypeStruct((slots + 2,), jnp.int32), jax.Sh...  2.91 us
  transfers between devices with their start and end apart: 6, of which 5 were waited for; matrix products, arithmetic and copies ran while one was open for 0% of the time, Pallas kernels for 11%

profile of v2, /device:TPU:1, one launch (start us, length us, event | category | flops | bytes accessed | tf_op | source)
XLA Modules:
  0.0 55.4 jit_solution(4427891693290214399)
XLA Ops:
  0.0 4.4 %collective-permute-start = (bf16[512,256]{1,0:T(8,128)(2,1)}, bf16[512,256]{1,0:T(8,128)(2,1)S(1)}, u32[]{:S(2)}, u32[]{:S(2)}) collective-permute-start(bf16[512,256]{1,0:T(8,128)(2,1)} %bitcast.3), channel_id=1, source_target_pairs={{0,4},{4,8},{8,12},{12,16},{16,20},{20,24},{24,28},{28,32},{32,36}... | collective-permute-start | bytes 786440 | tf_op jit(solution)/shard_map/ppermute | solution.py:23
  4.4 12.7 %collective-permute-start.2 = (bf16[512,256]{1,0:T(8,128)(2,1)}, bf16[512,256]{1,0:T(8,128)(2,1)S(1)}, u32[]{:S(2)}, u32[]{:S(2)}) collective-permute-start(bf16[512,256]{1,0:T(8,128)(2,1)} %bitcast.4), channel_id=1, source_target_pairs={{0,508},{4,0},{8,4},{12,8},{16,12},{20,16},{24,20},{28,24},{32,28}... | collective-permute-start | bytes 786440 | tf_op jit(solution)/shard_map/ppermute | solution.py:23
  17.1 2.9 %shard_map.64 = (s32[10]{0:T(128)S(1)}, bf16[512,256]{1,0:T(8,128)(2,1)S(1)}, bf16[8,256,1024]{2,1,0:T(8,128)(2,1)S(1)}) custom-call(s32[1024]{0:T(1024)} %cd_hbm.1, s32[128]{0:T(128)} %live_hbm.1, bf16[512,256]{1,0:T(8,128)(2,1)} %bitcast.5, bf16[8,256,1024]{2,1,0:T(8,128)(2,1)} %integrals_hbm.1), custom_call_target="tpu_custom_call" | custom-call | bytes 4194304 | tf_op jit(solution)/shard_map/pallas_call | solution.py:177
  20.0 1.4 %collective-permute-done.value_ref = bf16[512,256]{1,0:T(8,128)(2,1)S(1)} collective-permute-done((bf16[512,256]{1,0:T(8,128)(2,1)}, bf16[512,256]{1,0:T(8,128)(2,1)S(1)}, u32[]{:S(2)}, u32[]{:S(2)}) %collective-permute-start) | collective-permute-done | bytes 262176 | tf_op jit(solution)/shard_map/ppermute | solution.py:23
  21.4 1.9 %collective-permute-start.1 = (bf16[512,256]{1,0:T(8,128)(2,1)S(1)}, bf16[512,256]{1,0:T(8,128)(2,1)S(1)}, u32[]{:S(2)}, u32[]{:S(2)}) collective-permute-start(bf16[512,256]{1,0:T(8,128)(2,1)S(1)} %shard_map.65.refs_2_), channel_id=1, source_target_pairs={{0,4},{4,8},{8,12},{12,16},{16,20},{20,24},{24,28},{28,32},{32,36}... | collective-permute-start | bytes 786440 | tf_op jit(solution)/shard_map/ppermute | solution.py:23
  23.3 0.0 collective-permute-done.2.value_ref
  23.3 7.6 %collective-permute-start.3 = (bf16[512,256]{1,0:T(8,128)(2,1)S(1)}, bf16[512,256]{1,0:T(8,128)(2,1)S(1)}, u32[]{:S(2)}, u32[]{:S(2)}) collective-permute-start(bf16[512,256]{1,0:T(8,128)(2,1)S(1)} %shard_map.66.refs_3_), channel_id=1, source_target_pairs={{0,508},{4,0},{8,4},{12,8},{16,12},{20,16},{24,20},{28,24},{32,28}... | collective-permute-start | bytes 786440 | tf_op jit(solution)/shard_map/ppermute | solution.py:23
  30.9 1.7 %shard_map.67 = (f32[256,1024]{1,0:T(8,128)S(1)}, f32[256,1024]{1,0:T(8,128)S(1)}) custom-call(s32[10]{0:T(128)S(1)} %get-tuple-element.10.token_ref.refs_0_, bf16[8,256,1024]{2,1,0:T(8,128)(2,1)S(1)} %get-tuple-element.11.refs_1_, bf16[512,256]{1,0:T(8,128)(2,1)S(1)} %shard_map.65.refs_2_, bf16[512,256]{1,0:T(8,128)(2,1)S(1)} %shard_map.66.refs_3_, ...), custom_call_target="tpu_custom_call" | custom-call | flops 805306368 | tf_op jit(solution)/shard_map/pallas_call | solution.py:127
  32.7 1.4 %collective-permute-done.1.refs_2_ = bf16[512,256]{1,0:T(8,128)(2,1)S(1)} collective-permute-done((bf16[512,256]{1,0:T(8,128)(2,1)S(1)}, bf16[512,256]{1,0:T(8,128)(2,1)S(1)}, u32[]{:S(2)}, u32[]{:S(2)}) %collective-permute-start.1) | collective-permute-done | bytes 262176 | tf_op jit(solution)/shard_map/ppermute | solution.py:23
  34.1 0.9 %collective-permute-done.3.refs_3_ = bf16[512,256]{1,0:T(8,128)(2,1)S(1)} collective-permute-done((bf16[512,256]{1,0:T(8,128)(2,1)S(1)}, bf16[512,256]{1,0:T(8,128)(2,1)S(1)}, u32[]{:S(2)}, u32[]{:S(2)}) %collective-permute-start.3) | collective-permute-done | bytes 262176 | tf_op jit(solution)/shard_map/ppermute | solution.py:23
  35.0 1.6 %shard_map.68.refs_5_ = f32[256,1024]{1,0:T(8,128)S(1)} custom-call(s32[10]{0:T(128)S(1)} %get-tuple-element.10.token_ref.refs_0_, bf16[8,256,1024]{2,1,0:T(8,128)(2,1)S(1)} %get-tuple-element.11.refs_1_, bf16[512,256]{1,0:T(8,128)(2,1)S(1)} %collective-permute-done.1.refs_2_, bf16[512,256]{1,0:T(8,128)(2,1)S(1)} %collective-permute-done.3.refs_3_, ...), custom_call_target="tpu_custom_call" | custom-call | flops 402653184 | tf_op jit(solution)/shard_map/pallas_call | solution.py:127
  36.6 4.3 %collective-permute-start.4 = (f32[256,1024]{1,0:T(8,128)S(1)}, f32[256,1024]{1,0:T(8,128)S(1)}, u32[]{:S(2)}, u32[]{:S(2)}) collective-permute-start(f32[256,1024]{1,0:T(8,128)S(1)} %shard_map.68.refs_5_), channel_id=1, source_target_pairs={{0,1},{1,0},{2,3},{3,2},{4,5},{5,4},{6,7},{7,6},{8,9},{9,8},{10,11... | collective-permute-start | bytes 3145736 | tf_op jit(solution)/shard_map/ppermute | solution.py:165
  41.0 0.0 copy-start.1
  41.0 0.0 copy-start
  41.0 1.6 %shard_map.69.mine_ref = f32[256,1024]{1,0:T(8,128)S(1)} custom-call(s32[10]{0:T(128)S(1)} %get-tuple-element.10.token_ref.refs_0_, bf16[8,256,1024]{2,1,0:T(8,128)(2,1)S(1)} %get-tuple-element.11.refs_1_, bf16[512,256]{1,0:T(8,128)(2,1)S(1)} %collective-permute-done.1.refs_2_, bf16[512,256]{1,0:T(8,128)(2,1)S(1)} %collective-permute-done.3.refs_3_, ...), custom_call_target="tpu_custom_call" | custom-call | flops 402653184 | tf_op jit(solution)/shard_map/pallas_call | solution.py:127
  42.6 0.6 %collective-permute-done.4.arrived_ref = f32[256,1024]{1,0:T(8,128)S(1)} collective-permute-done((f32[256,1024]{1,0:T(8,128)S(1)}, f32[256,1024]{1,0:T(8,128)S(1)}, u32[]{:S(2)}, u32[]{:S(2)}) %collective-permute-start.4) | collective-permute-done | bytes 1048608 | tf_op jit(solution)/shard_map/ppermute | solution.py:165
  43.2 0.2 shard_map.70
  43.4 4.5 %collective-permute-start.5 = (s16[1040,128]{1,0:T(8,128)(2,1)S(1)}, s16[1040,128]{1,0:T(8,128)(2,1)S(1)}, u32[]{:S(2)}, u32[]{:S(2)}) collective-permute-start(s16[1040,128]{1,0:T(8,128)(2,1)S(1)} %shard_map.70), channel_id=1, source_target_pairs={{0,2},{1,3},{2,0},{3,1},{4,6},{5,7},{6,4},{7,5},{8,10},{9,11},{10,... | collective-permute-start | bytes 798728 | tf_op jit(solution)/shard_map/ppermute | solution.py:169
  47.9 0.0 copy-done.1
  48.0 0.1 copy.9.occ_ref
  48.1 6.3 %collective-permute-done.5.code_ref = s16[1040,128]{1,0:T(8,128)(2,1)S(1)} collective-permute-done((s16[1040,128]{1,0:T(8,128)(2,1)S(1)}, s16[1040,128]{1,0:T(8,128)(2,1)S(1)}, u32[]{:S(2)}, u32[]{:S(2)}) %collective-permute-start.5) | collective-permute-done | bytes 266272 | tf_op jit(solution)/shard_map/ppermute | solution.py:169
  54.4 0.0 copy-done
  54.4 1.0 %shard_map.71 = f32[128,1024]{1,0:T(8,128)} custom-call(f32[256,1024]{1,0:T(8,128)S(1)} %shard_map.69.mine_ref, f32[256,1024]{1,0:T(8,128)S(1)} %collective-permute-done.4.arrived_ref, s16[1040,128]{1,0:T(8,128)(2,1)S(1)} %collective-permute-done.5.code_ref, f32[128,1]{1,0:T(8,128)S(1)} %copy.9.occ_ref, f32[1,1024]{1,0:T(1,128)S(1)} %copy-done), custom_call_target="tpu_custom_call" | custom-call | bytes 1048576 | tf_op jit(solution)/shard_map/pallas_call | solution.py:204
  (2 shorter events, 0.0 us)
Async XLA Ops:
  0.0 21.4 %collective-permute-start = (bf16[512,256]{1,0:T(8,128)(2,1)}, bf16[512,256]{1,0:T(8,128)(2,1)S(1)}, u32[]{:S(2)}, u32[]{:S(2)}) collective-permute-start(bf16[512,256]{1,0:T(8,128)(2,1)} %bitcast.3), channel_id=1, source_target_pairs={{0,4},{4,8},{8,12},{12,16},{16,20},{20,24},{24,28},{28,32},{32,36}... | collective-permute-start | bytes 786440 | tf_op jit(solution)/shard_map/ppermute | solution.py:23
  4.4 18.9 %collective-permute-start.2 = (bf16[512,256]{1,0:T(8,128)(2,1)}, bf16[512,256]{1,0:T(8,128)(2,1)S(1)}, u32[]{:S(2)}, u32[]{:S(2)}) collective-permute-start(bf16[512,256]{1,0:T(8,128)(2,1)} %bitcast.4), channel_id=1, source_target_pairs={{0,508},{4,0},{8,4},{12,8},{16,12},{20,16},{24,20},{28,24},{32,28}... | collective-permute-start | bytes 786440 | tf_op jit(solution)/shard_map/ppermute | solution.py:23
  21.4 12.7 %collective-permute-start.1 = (bf16[512,256]{1,0:T(8,128)(2,1)S(1)}, bf16[512,256]{1,0:T(8,128)(2,1)S(1)}, u32[]{:S(2)}, u32[]{:S(2)}) collective-permute-start(bf16[512,256]{1,0:T(8,128)(2,1)S(1)} %shard_map.65.refs_2_), channel_id=1, source_target_pairs={{0,4},{4,8},{8,12},{12,16},{16,20},{20,24},{24,28},{28,32},{32,36}... | collective-permute-start | bytes 786440 | tf_op jit(solution)/shard_map/ppermute | solution.py:23
  23.3 11.7 %collective-permute-start.3 = (bf16[512,256]{1,0:T(8,128)(2,1)S(1)}, bf16[512,256]{1,0:T(8,128)(2,1)S(1)}, u32[]{:S(2)}, u32[]{:S(2)}) collective-permute-start(bf16[512,256]{1,0:T(8,128)(2,1)S(1)} %shard_map.66.refs_3_), channel_id=1, source_target_pairs={{0,508},{4,0},{8,4},{12,8},{16,12},{20,16},{24,20},{28,24},{32,28}... | collective-permute-start | bytes 786440 | tf_op jit(solution)/shard_map/ppermute | solution.py:23
  36.6 6.6 %collective-permute-start.4 = (f32[256,1024]{1,0:T(8,128)S(1)}, f32[256,1024]{1,0:T(8,128)S(1)}, u32[]{:S(2)}, u32[]{:S(2)}) collective-permute-start(f32[256,1024]{1,0:T(8,128)S(1)} %shard_map.68.refs_5_), channel_id=1, source_target_pairs={{0,1},{1,0},{2,3},{3,2},{4,5},{5,4},{6,7},{7,6},{8,9},{9,8},{10,11... | collective-permute-start | bytes 3145736 | tf_op jit(solution)/shard_map/ppermute | solution.py:165
  41.0 7.0 %copy-start.1 = (f32[128]{0:T(128)S(1)}, f32[128]{0:T(128)}, u32[]{:S(2)}) copy-start(f32[128]{0:T(128)} %param.10) | copy-start | bytes 1540
  41.0 13.4 %copy-start = (f32[1,1024]{1,0:T(1,128)S(1)}, f32[1,1024]{1,0:T(1,128)}, u32[]{:S(2)}) copy-start(f32[1,1024]{1,0:T(1,128)} %vir_ref.1) | copy-start | bytes 12292
  43.4 11.0 %collective-permute-start.5 = (s16[1040,128]{1,0:T(8,128)(2,1)S(1)}, s16[1040,128]{1,0:T(8,128)(2,1)S(1)}, u32[]{:S(2)}, u32[]{:S(2)}) collective-permute-start(s16[1040,128]{1,0:T(8,128)(2,1)S(1)} %shard_map.70), channel_id=1, source_target_pairs={{0,2},{1,3},{2,0},{3,1},{4,6},{5,7},{6,4},{7,5},{8,10},{9,11},{10,... | collective-permute-start | bytes 798728 | tf_op jit(solution)/shard_map/ppermute | solution.py:169

commit v3 on v2

--- a/solution.py
+++ b/solution.py
@@ -54,45 +54,31 @@
     copies[3].wait()
 
 
-def gated(value, token):
+def gated(value, token, flops=0):
     return call(
         lambda value_ref, token_ref, out_ref: None,
         jax.ShapeDtypeStruct(value.shape, value.dtype),
         [ANY, ANY],
         ANY,
+        flops=flops,
         aliases={0: 0},
     )(value, token)
 
 
-def ladder_kernel(among, flips, pieces, plan_ref, integrals_ref, *refs):
-    count = len(among) * pieces
-    sources, rest = refs[:count], refs[count:]
-    out_count = len(flips)
+def ladder_kernel(among, flips, plan_ref, integrals_ref, *refs):
+    sources, rest = refs[: len(among)], refs[len(among) :]
     near_ref = rest[-1]
-    outs = rest[-1 - out_count : -1]
-    starts = rest[: len(rest) - 1 - out_count]
+    outs = rest[-1 - len(flips) : -1]
+    starts = rest[: len(rest) - 1 - len(flips)]
     slots, depth, width = integrals_ref.shape
-    height = outs[0].shape[0] // 2
+    height = outs[0].shape[0]
     high, core = plan_ref[slots], plan_ref[slots + 1]
-    for which, group in enumerate(flips):
-        for at, (flip_high, flip_core) in enumerate(group):
-            block_high = 1 - high if flip_high else high
-            block_core = 1 - core if flip_core else core
-            target = slice((2 * which + at) * height, (2 * which + at + 1) * height)
-            for index in range(len(among)):
-                if pieces == 1:
-                    rows = pl.ds(pl.multiple_of((2 * block_high + block_core) * height, height), height)
-                    near_ref[index, target, :] = sources[index][rows, :]
-                else:
-                    rows = pl.ds(pl.multiple_of(block_core * height, height), height)
-                    for piece in range(2):
-
-                        @pl.when(block_high == piece)
-                        def _():
-                            near_ref[index, target, :] = sources[2 * index + piece][rows, :]
-
-    for which, out in enumerate(outs):
-        out[...] = starts[which][...] if starts else jnp.zeros_like(out)
+    for at, (flip_high, flip_core) in enumerate(flips):
+        block = 2 * (1 - high if flip_high else high) + (1 - core if flip_core else core)
+        rows = pl.ds(pl.multiple_of(block * height, height), height)
+        for index, source in enumerate(sources):
+            near_ref[index, at * height : (at + 1) * height, :] = source[rows, :]
+        outs[at][...] = starts[at][...] if starts else jnp.zeros_like(outs[at])
 
     def one_slot(slot, carry):
         offset = plan_ref[slot]
@@ -104,42 +90,42 @@
         @pl.when(wanted)
         def _():
             for column in range(0, width, 256):
-                matrix = integrals_ref[slot, :, column : column + 256]
-                for which, out in enumerate(outs):
-                    amp = near_ref[index, 2 * which * height : 2 * (which + 1) * height, :]
-                    out[:, column : column + 256] += jnp.dot(amp, matrix, preferred_element_type=jnp.float32)
+                columns = slice(column, column + 256)
+                product = jnp.dot(
+                    near_ref[index, :, :], integrals_ref[slot, :, columns], preferred_element_type=jnp.float32
+                )
+                for at, out in enumerate(outs):
+                    out[:, columns] += product[at * height : (at + 1) * height, :]
 
         return carry
 
     lax.fori_loop(0, slots, one_slot, 0)
 
 
-SEND = ((True, True), (False, True))
-MINE = ((True, False), (False, False))
+FAR_SEND, FAR_MINE, NEAR_SEND, NEAR_MINE = (True, True), (True, False), (False, True), (False, False)
 
 
 def ladder(among, flips, plan, integrals, blocks, starts=(), after=()):
     slots, depth, width = integrals.shape
-    pieces = len(blocks) // len(among)
-    height = blocks[0].shape[0] * pieces // 4
-    row_count = 2 * height * len(flips)
-    out = (jax.ShapeDtypeStruct((2 * height, width), jnp.float32),) * len(flips)
+    height = blocks[0].shape[0] // 4
+    outs = (jax.ShapeDtypeStruct((height, width), jnp.float32),) * len(flips)
+    used = 2 + len(among) + len(starts)
     return call(
-        lambda *refs: ladder_kernel(among, flips, pieces, *(refs[: len(refs) - 1 - len(flips) - len(after)] + refs[len(refs) - 1 - len(flips) :])),
-        out,
-        [SMEM] + [VMEM] * (1 + len(blocks) + len(starts)) + [ANY] * len(after),
+        lambda *refs: ladder_kernel(among, flips, *refs[:used], *refs[used + len(after) :]),
+        outs,
+        [SMEM] + [VMEM] * (used - 1) + [ANY] * len(after),
         (VMEM,) * len(flips),
-        [pltpu.VMEM((len(among), row_count, depth), blocks[0].dtype)],
-        2 * 3 * row_count * depth * width,
+        [pltpu.VMEM((len(among), height * len(flips), depth), blocks[0].dtype)],
+        2 * 3 * height * len(flips) * depth * width,
     )(plan, integrals, *blocks, *starts, *after)
 
 
 def encode_kernel(mine_ref, arrived_ref, code_ref):
-    height, width = mine_ref.shape[0] // 2, mine_ref.shape[1]
+    height, width = mine_ref.shape
     marks = []
     for chunk in range(width // 128):
         columns = slice(chunk * 128, (chunk + 1) * 128)
-        value = mine_ref[:height, columns] + arrived_ref[:height, columns]
+        value = mine_ref[:, columns] + arrived_ref[:, columns]
         peak = jnp.maximum(jnp.max(jnp.abs(value), axis=0, keepdims=True), LEAST_PEAK)
         mark = jnp.ceil(jnp.log2(peak) * LOG_STEPS)
         marks.append(mark)
@@ -157,7 +143,7 @@
     for chunk in range(chunks):
         columns = slice(chunk * 128, (chunk + 1) * 128)
         other = code_ref[chunk * height : (chunk + 1) * height, :].astype(jnp.int32).astype(jnp.float32)
-        total = mine_ref[height:, columns] + arrived_ref[height:, columns] + other * scales[chunk : chunk + 1, :]
+        total = mine_ref[:, columns] + arrived_ref[:, columns] + other * scales[chunk : chunk + 1, :]
         out_ref[:, columns] = total / (vir_ref[:, columns] - occ_ref[...])
 
 
@@ -192,18 +178,26 @@
     arrived[-2] = shifted(arrived[-1], "blk", 1)
     arrived[2] = shifted(arrived[1], "blk", -1)
     blocks = [arrived[step] if step else own_here for step in range(-REACH, REACH + 1)]
-    first_send, first_mine = ladder((1, 3, 2), (SEND, MINE), plan, integrals_here, [blocks[at] for at in (1, 3, 2)])
-    (send,) = ladder((0, 4), (SEND,), plan, integrals_here, [blocks[at] for at in (0, 4)], (first_send,))
-    arrived_core = to_other_core(send)
-    (mine,) = ladder((0, 4), (MINE,), plan, integrals_here, [blocks[at] for at in (0, 4)], (first_mine,), (send,))
+    close, distant = (1, 3, 2), (0, 4)
+    close_blocks, distant_blocks = [blocks[at] for at in close], [blocks[at] for at in distant]
+    first = ladder(
+        close, (FAR_SEND, FAR_MINE, NEAR_SEND, NEAR_MINE), plan, integrals_here, close_blocks
+    )
+    (far_send,) = ladder(distant, (FAR_SEND,), plan, integrals_here, distant_blocks, first[:1])
+    far_arrived = to_other_core(far_send)
+    (far_mine,) = ladder(distant, (FAR_MINE,), plan, integrals_here, distant_blocks, first[1:2], (far_send,))
     chunks = width // 128
     code = call(
         encode_kernel, jax.ShapeDtypeStruct((chunks * height + 16, 128), jnp.int16), [VMEM] * 2, VMEM, (), 0, 1 << 20
-    )(mine, arrived_core)
-    code_arrived = to_other_chip(code)
+    )(far_mine, far_arrived)
+    code_arrived = gated(to_other_chip(code), plan, 4 * 10**9)
+    near_send, near_mine = ladder(
+        distant, (NEAR_SEND, NEAR_MINE), plan, integrals_here, distant_blocks, first[2:], (code,)
+    )
+    near_arrived = to_other_core(near_send)
     out = call(
         finish_kernel, jax.ShapeDtypeStruct((height, width), jnp.float32), [VMEM] * 5, VMEM, (), 0, 1 << 20
-    )(mine, arrived_core, code_arrived, occ_energy[:, None], vir_energy)
+    )(near_mine, near_arrived, code_arrived, occ_energy[:, None], vir_energy)
     return out[None]
 
 

time: 55.7 us -> 54.5 us (0.978)
  waiting for transfers between devices: 10.6 us -> 6.02 us
  starting transfers between devices: 35.4 us -> 38 us
  Pallas kernels: 9.11 us -> 9.93 us
    ppermute x1, waiting for transfers between devices: 6.35 us -> 2.41 us  [to_other_chip(): return lax.ppermute(value, 'grp', [(0, 2), (1, 3), (2, 0), (3, 1)])]
    ppermute x1 -> x2, starting transfers between devices: 4.34 us -> 6.9 us  [to_other_core(): return lax.ppermute(value, 'grp', [(0, 1), (1, 0), (2, 3), (3, 2)])]
    pallas_call x3 -> x4, Pallas kernels: 5.03 us -> 5.85 us  [ladder(): call(lambda *refs: ladder_kernel(among, flips, *refs[:used], *refs[used +...]
  transfers between devices with their start and end apart: 6 -> 7, of which waited for: 5 -> 5; matrix products, arithmetic and copies ran while one was open for 0% -> 0% of each run, Pallas kernels for 11% -> 14%
where the time goes in v3:
time: 54.5 us; the launch traced here: 54.2 us
  starting transfers between devices  38 us (70%)
  Pallas kernels  9.93 us (18%)
  waiting for transfers between devices  6.02 us (11%)
    ppermute x4, starting transfers between devices, shifted(): return lax.ppermute(value, axis, pairs)  26.6 us
    ppermute x2, starting transfers between devices, to_other_core(): return lax.ppermute(value, 'grp', [(0, 1), (1, 0), (2, 3), (3, 2)])  6.9 us
    pallas_call x4, Pallas kernels, ladder(): call(lambda *refs: ladder_kernel(among, flips, *refs[:used], *refs[used +...  5.85 us
    ppermute x1, starting transfers between devices, to_other_chip(): return lax.ppermute(value, 'grp', [(0, 2), (1, 3), (2, 0), (3, 1)])  4.53 us
    ppermute x4, waiting for transfers between devices, shifted(): return lax.ppermute(value, axis, pairs)  3.28 us
    pallas_call x1, Pallas kernels, body(): call(fetch_kernel, (jax.ShapeDtypeStruct((slots + 2,), jnp.int32), jax.Sh...  2.91 us
    ppermute x1, waiting for transfers between devices, to_other_chip(): return lax.ppermute(value, 'grp', [(0, 2), (1, 3), (2, 0), (3, 1)])  2.41 us
  transfers between devices with their start and end apart: 7, of which 5 were waited for; matrix products, arithmetic and copies ran while one was open for 0% of the time, Pallas kernels for 14%

profile of v3, /device:TPU:1, one launch (start us, length us, event | category | flops | bytes accessed | tf_op | source)
XLA Modules:
  0.0 54.2 jit_solution(17025446429573779424)
XLA Ops:
  0.0 4.4 %collective-permute-start = (bf16[512,256]{1,0:T(8,128)(2,1)}, bf16[512,256]{1,0:T(8,128)(2,1)S(1)}, u32[]{:S(2)}, u32[]{:S(2)}) collective-permute-start(bf16[512,256]{1,0:T(8,128)(2,1)} %bitcast.3), channel_id=1, source_target_pairs={{0,4},{4,8},{8,12},{12,16},{16,20},{20,24},{24,28},{28,32},{32,36}... | collective-permute-start | bytes 786440 | tf_op jit(solution)/shard_map/ppermute | solution.py:23
  4.4 12.7 %collective-permute-start.2 = (bf16[512,256]{1,0:T(8,128)(2,1)}, bf16[512,256]{1,0:T(8,128)(2,1)S(1)}, u32[]{:S(2)}, u32[]{:S(2)}) collective-permute-start(bf16[512,256]{1,0:T(8,128)(2,1)} %bitcast.4), channel_id=1, source_target_pairs={{0,508},{4,0},{8,4},{12,8},{16,12},{20,16},{24,20},{28,24},{32,28}... | collective-permute-start | bytes 786440 | tf_op jit(solution)/shard_map/ppermute | solution.py:23
  17.1 2.9 %shard_map.64 = (s32[10]{0:T(128)S(1)}, bf16[512,256]{1,0:T(8,128)(2,1)S(1)}, bf16[8,256,1024]{2,1,0:T(8,128)(2,1)S(1)}) custom-call(s32[1024]{0:T(1024)} %cd_hbm.1, s32[128]{0:T(128)} %live_hbm.1, bf16[512,256]{1,0:T(8,128)(2,1)} %bitcast.5, bf16[8,256,1024]{2,1,0:T(8,128)(2,1)} %integrals_hbm.1), custom_call_target="tpu_custom_call" | custom-call | bytes 4194304 | tf_op jit(solution)/shard_map/pallas_call | solution.py:163
  20.0 1.4 %collective-permute-done.value_ref = bf16[512,256]{1,0:T(8,128)(2,1)S(1)} collective-permute-done((bf16[512,256]{1,0:T(8,128)(2,1)}, bf16[512,256]{1,0:T(8,128)(2,1)S(1)}, u32[]{:S(2)}, u32[]{:S(2)}) %collective-permute-start) | collective-permute-done | bytes 262176 | tf_op jit(solution)/shard_map/ppermute | solution.py:23
  21.4 1.9 %collective-permute-start.1 = (bf16[512,256]{1,0:T(8,128)(2,1)S(1)}, bf16[512,256]{1,0:T(8,128)(2,1)S(1)}, u32[]{:S(2)}, u32[]{:S(2)}) collective-permute-start(bf16[512,256]{1,0:T(8,128)(2,1)S(1)} %shard_map.65.refs_2_), channel_id=1, source_target_pairs={{0,4},{4,8},{8,12},{12,16},{16,20},{20,24},{24,28},{28,32},{32,36}... | collective-permute-start | bytes 786440 | tf_op jit(solution)/shard_map/ppermute | solution.py:23
  23.3 0.0 collective-permute-done.2.value_ref
  23.3 7.6 %collective-permute-start.3 = (bf16[512,256]{1,0:T(8,128)(2,1)S(1)}, bf16[512,256]{1,0:T(8,128)(2,1)S(1)}, u32[]{:S(2)}, u32[]{:S(2)}) collective-permute-start(bf16[512,256]{1,0:T(8,128)(2,1)S(1)} %shard_map.66.refs_3_), channel_id=1, source_target_pairs={{0,508},{4,0},{8,4},{12,8},{16,12},{20,16},{24,20},{28,24},{32,28}... | collective-permute-start | bytes 786440 | tf_op jit(solution)/shard_map/ppermute | solution.py:23
  30.9 2.2 %shard_map.67 = (f32[128,1024]{1,0:T(8,128)S(1)}, f32[128,1024]{1,0:T(8,128)S(1)}, f32[128,1024]{1,0:T(8,128)S(1)}, f32[128,1024]{1,0:T(8,128)S(1)}) custom-call(s32[10]{0:T(128)S(1)} %get-tuple-element.14.token_ref.refs_0_, bf16[8,256,1024]{2,1,0:T(8,128)(2,1)S(1)} %get-tuple-element.15.refs_1_, bf16[512,256]{1,0:T(8,128)(2,1)S(1)} %shard_map.65.refs_2_, ...), custom_call_target="tpu_custom_call" | custom-call | flops 805306368 | tf_op jit(solution)/shard_map/pallas_call | solution.py:113
  33.1 1.0 %collective-permute-done.1.refs_2_ = bf16[512,256]{1,0:T(8,128)(2,1)S(1)} collective-permute-done((bf16[512,256]{1,0:T(8,128)(2,1)S(1)}, bf16[512,256]{1,0:T(8,128)(2,1)S(1)}, u32[]{:S(2)}, u32[]{:S(2)}) %collective-permute-start.1) | collective-permute-done | bytes 262176 | tf_op jit(solution)/shard_map/ppermute | solution.py:23
  34.1 0.9 %collective-permute-done.3.refs_3_ = bf16[512,256]{1,0:T(8,128)(2,1)S(1)} collective-permute-done((bf16[512,256]{1,0:T(8,128)(2,1)S(1)}, bf16[512,256]{1,0:T(8,128)(2,1)S(1)}, u32[]{:S(2)}, u32[]{:S(2)}) %collective-permute-start.3) | collective-permute-done | bytes 262176 | tf_op jit(solution)/shard_map/ppermute | solution.py:23
  35.0 1.2 %shard_map.68.refs_5_ = f32[128,1024]{1,0:T(8,128)S(1)} custom-call(s32[10]{0:T(128)S(1)} %get-tuple-element.14.token_ref.refs_0_, bf16[8,256,1024]{2,1,0:T(8,128)(2,1)S(1)} %get-tuple-element.15.refs_1_, bf16[512,256]{1,0:T(8,128)(2,1)S(1)} %collective-permute-done.1.refs_2_, bf16[512,256]{1,0:T(8,128)(2,1)S(1)} %collective-permute-done.3.refs_3_, ...), custom_call_target="tpu_custom_call" | custom-call | flops 201326592 | tf_op jit(solution)/shard_map/pallas_call | solution.py:113
  36.2 4.3 %collective-permute-start.4 = (f32[128,1024]{1,0:T(8,128)S(1)}, f32[128,1024]{1,0:T(8,128)S(1)}, u32[]{:S(2)}, u32[]{:S(2)}) collective-permute-start(f32[128,1024]{1,0:T(8,128)S(1)} %shard_map.68.refs_5_), channel_id=1, source_target_pairs={{0,1},{1,0},{2,3},{3,2},{4,5},{5,4},{6,7},{7,6},{8,9},{9,8},{10,11... | collective-permute-start | bytes 1572872 | tf_op jit(solution)/shard_map/ppermute | solution.py:151
  40.5 1.2 %shard_map.69.mine_ref = f32[128,1024]{1,0:T(8,128)S(1)} custom-call(s32[10]{0:T(128)S(1)} %get-tuple-element.14.token_ref.refs_0_, bf16[8,256,1024]{2,1,0:T(8,128)(2,1)S(1)} %get-tuple-element.15.refs_1_, bf16[512,256]{1,0:T(8,128)(2,1)S(1)} %collective-permute-done.1.refs_2_, bf16[512,256]{1,0:T(8,128)(2,1)S(1)} %collective-permute-done.3.refs_3_, ...), custom_call_target="tpu_custom_call" | custom-call | flops 201326592 | tf_op jit(solution)/shard_map/pallas_call | solution.py:113
  41.7 0.0 copy-start.1
  41.7 0.3 collective-permute-done.4.arrived_ref
  42.0 0.2 shard_map.70.refs_6_
  42.2 4.5 %collective-permute-start.6 = (s16[1040,128]{1,0:T(8,128)(2,1)S(1)}, s16[1040,128]{1,0:T(8,128)(2,1)S(1)}, u32[]{:S(2)}, u32[]{:S(2)}) collective-permute-start(s16[1040,128]{1,0:T(8,128)(2,1)S(1)} %shard_map.70.refs_6_), channel_id=1, source_target_pairs={{0,2},{1,3},{2,0},{3,1},{4,6},{5,7},{6,4},{7,5},{8,10},{9,11},{10,... | collective-permute-start | bytes 798728 | tf_op jit(solution)/shard_map/ppermute | solution.py:155
  46.7 1.3 %shard_map.71 = (f32[128,1024]{1,0:T(8,128)S(1)}, f32[128,1024]{1,0:T(8,128)S(1)}) custom-call(s32[10]{0:T(128)S(1)} %get-tuple-element.14.token_ref.refs_0_, bf16[8,256,1024]{2,1,0:T(8,128)(2,1)S(1)} %get-tuple-element.15.refs_1_, bf16[512,256]{1,0:T(8,128)(2,1)S(1)} %collective-permute-done.1.refs_2_, bf16[512,256]{1,0:T(8,128)(2,1)S(1)} %collective-permute-done.3.refs_3_, ...), custom_call_target="tpu_custom_call" | custom-call | flops 402653184 | tf_op jit(solution)/shard_map/pallas_call | solution.py:113
  48.1 2.6 %collective-permute-start.5 = (f32[128,1024]{1,0:T(8,128)S(1)}, f32[128,1024]{1,0:T(8,128)S(1)}, u32[]{:S(2)}, u32[]{:S(2)}) collective-permute-start(f32[128,1024]{1,0:T(8,128)S(1)} %get-tuple-element.22), channel_id=1, source_target_pairs={{0,1},{1,0},{2,3},{3,2},{4,5},{5,4},{6,7},{7,6},{8,9},{9,8},{10,11... | collective-permute-start | bytes 1572872 | tf_op jit(solution)/shard_map/ppermute | solution.py:151
  50.6 0.0 copy-done.1
  50.7 0.1 copy.10.occ_ref
  50.8 0.0 copy-start
  50.8 2.4 %collective-permute-done.6.value_ref = s16[1040,128]{1,0:T(8,128)(2,1)S(1)} collective-permute-done((s16[1040,128]{1,0:T(8,128)(2,1)S(1)}, s16[1040,128]{1,0:T(8,128)(2,1)S(1)}, u32[]{:S(2)}, u32[]{:S(2)}) %collective-permute-start.6) | collective-permute-done | bytes 266272 | tf_op jit(solution)/shard_map/ppermute | solution.py:155
  53.2 0.0 collective-permute-done.5.arrived_ref
  53.2 0.0 copy-done
  53.2 1.0 %shard_map.73 = f32[128,1024]{1,0:T(8,128)} custom-call(f32[128,1024]{1,0:T(8,128)S(1)} %get-tuple-element.21.mine_ref, f32[128,1024]{1,0:T(8,128)S(1)} %collective-permute-done.5.arrived_ref, s16[1040,128]{1,0:T(8,128)(2,1)S(1)} %shard_map.72.code_ref, f32[128,1]{1,0:T(8,128)S(1)} %copy.10.occ_ref, f32[1,1024]{1,0:T(1,128)S(1)} %copy-done), custom_call_target="tpu_custom_call" | custom-call | bytes 1048576 | tf_op jit(solution)/shard_map/pallas_call | solution.py:198
  (3 shorter events, 0.0 us)
Async XLA Ops:
  0.0 21.4 %collective-permute-start = (bf16[512,256]{1,0:T(8,128)(2,1)}, bf16[512,256]{1,0:T(8,128)(2,1)S(1)}, u32[]{:S(2)}, u32[]{:S(2)}) collective-permute-start(bf16[512,256]{1,0:T(8,128)(2,1)} %bitcast.3), channel_id=1, source_target_pairs={{0,4},{4,8},{8,12},{12,16},{16,20},{20,24},{24,28},{28,32},{32,36}... | collective-permute-start | bytes 786440 | tf_op jit(solution)/shard_map/ppermute | solution.py:23
  4.4 18.9 %collective-permute-start.2 = (bf16[512,256]{1,0:T(8,128)(2,1)}, bf16[512,256]{1,0:T(8,128)(2,1)S(1)}, u32[]{:S(2)}, u32[]{:S(2)}) collective-permute-start(bf16[512,256]{1,0:T(8,128)(2,1)} %bitcast.4), channel_id=1, source_target_pairs={{0,508},{4,0},{8,4},{12,8},{16,12},{20,16},{24,20},{28,24},{32,28}... | collective-permute-start | bytes 786440 | tf_op jit(solution)/shard_map/ppermute | solution.py:23
  21.4 12.7 %collective-permute-start.1 = (bf16[512,256]{1,0:T(8,128)(2,1)S(1)}, bf16[512,256]{1,0:T(8,128)(2,1)S(1)}, u32[]{:S(2)}, u32[]{:S(2)}) collective-permute-start(bf16[512,256]{1,0:T(8,128)(2,1)S(1)} %shard_map.65.refs_2_), channel_id=1, source_target_pairs={{0,4},{4,8},{8,12},{12,16},{16,20},{20,24},{24,28},{28,32},{32,36}... | collective-permute-start | bytes 786440 | tf_op jit(solution)/shard_map/ppermute | solution.py:23
  23.3 11.7 %collective-permute-start.3 = (bf16[512,256]{1,0:T(8,128)(2,1)S(1)}, bf16[512,256]{1,0:T(8,128)(2,1)S(1)}, u32[]{:S(2)}, u32[]{:S(2)}) collective-permute-start(bf16[512,256]{1,0:T(8,128)(2,1)S(1)} %shard_map.66.refs_3_), channel_id=1, source_target_pairs={{0,508},{4,0},{8,4},{12,8},{16,12},{20,16},{24,20},{28,24},{32,28}... | collective-permute-start | bytes 786440 | tf_op jit(solution)/shard_map/ppermute | solution.py:23
  36.2 5.9 %collective-permute-start.4 = (f32[128,1024]{1,0:T(8,128)S(1)}, f32[128,1024]{1,0:T(8,128)S(1)}, u32[]{:S(2)}, u32[]{:S(2)}) collective-permute-start(f32[128,1024]{1,0:T(8,128)S(1)} %shard_map.68.refs_5_), channel_id=1, source_target_pairs={{0,1},{1,0},{2,3},{3,2},{4,5},{5,4},{6,7},{7,6},{8,9},{9,8},{10,11... | collective-permute-start | bytes 1572872 | tf_op jit(solution)/shard_map/ppermute | solution.py:151
  41.7 9.0 %copy-start.1 = (f32[128]{0:T(128)S(1)}, f32[128]{0:T(128)}, u32[]{:S(2)}) copy-start(f32[128]{0:T(128)} %param.10) | copy-start | bytes 1540
  42.2 11.0 %collective-permute-start.6 = (s16[1040,128]{1,0:T(8,128)(2,1)S(1)}, s16[1040,128]{1,0:T(8,128)(2,1)S(1)}, u32[]{:S(2)}, u32[]{:S(2)}) collective-permute-start(s16[1040,128]{1,0:T(8,128)(2,1)S(1)} %shard_map.70.refs_6_), channel_id=1, source_target_pairs={{0,2},{1,3},{2,0},{3,1},{4,6},{5,7},{6,4},{7,5},{8,10},{9,11},{10,... | collective-permute-start | bytes 798728 | tf_op jit(solution)/shard_map/ppermute | solution.py:155
  48.1 5.1 %collective-permute-start.5 = (f32[128,1024]{1,0:T(8,128)S(1)}, f32[128,1024]{1,0:T(8,128)S(1)}, u32[]{:S(2)}, u32[]{:S(2)}) collective-permute-start(f32[128,1024]{1,0:T(8,128)S(1)} %get-tuple-element.22), channel_id=1, source_target_pairs={{0,1},{1,0},{2,3},{3,2},{4,5},{5,4},{6,7},{7,6},{8,9},{9,8},{10,11... | collective-permute-start | bytes 1572872 | tf_op jit(solution)/shard_map/ppermute | solution.py:151
  50.8 2.4 %copy-start = (f32[1,1024]{1,0:T(1,128)S(1)}, f32[1,1024]{1,0:T(1,128)}, u32[]{:S(2)}) copy-start(f32[1,1024]{1,0:T(1,128)} %vir_ref.1) | copy-start | bytes 12292

commit v4 on v3

--- a/solution.py
+++ b/solution.py
@@ -6,6 +6,7 @@
 from jax.sharding import PartitionSpec as P
 
 REACH = 2
+RING = 16
 LEVELS = 32767.0
 LOG_STEPS = 128.0
 LEAST_PEAK = 2.0**-120
@@ -17,10 +18,10 @@
 HBM = pl.BlockSpec(memory_space=pltpu.HBM)
 
 
-def shifted(value, axis, steps):
-    count = lax.axis_size(axis)
+def shifted(value, steps, targets=None):
+    count = lax.axis_size("blk")
     pairs = [(source, (source + steps) % count) for source in range(count)]
-    return lax.ppermute(value, axis, pairs)
+    return lax.ppermute(value, "blk", [pair for pair in pairs if targets is None or pair[1] in targets])
 
 
 def call(kernel, out_shape, in_specs, out_specs, scratch=(), flops=0, moved=0, aliases={}):
@@ -50,6 +51,7 @@
         plan_ref[slot] = jnp.where(slot < live_ref[here], offset, -1)
     plan_ref[slots] = grp // 2
     plan_ref[slots + 1] = lax.rem(grp, 2)
+    plan_ref[slots + 2] = jnp.where(lax.rem(here, RING) == 0, 1, 0)
     copies[2].wait()
     copies[3].wait()
 
@@ -65,19 +67,28 @@
     )(value, token)
 
 
-def ladder_kernel(among, flips, plan_ref, integrals_ref, *refs):
-    sources, rest = refs[: len(among)], refs[len(among) :]
+def ladder_kernel(among, flips, source_count, plan_ref, integrals_ref, *refs):
+    sources, rest = refs[:source_count], refs[source_count:]
     near_ref = rest[-1]
     outs = rest[-1 - len(flips) : -1]
     starts = rest[: len(rest) - 1 - len(flips)]
     slots, depth, width = integrals_ref.shape
     height = outs[0].shape[0]
-    high, core = plan_ref[slots], plan_ref[slots + 1]
+    high, core, ring_start = plan_ref[slots], plan_ref[slots + 1], plan_ref[slots + 2]
     for at, (flip_high, flip_core) in enumerate(flips):
         block = 2 * (1 - high if flip_high else high) + (1 - core if flip_core else core)
         rows = pl.ds(pl.multiple_of(block * height, height), height)
-        for index, source in enumerate(sources):
-            near_ref[index, at * height : (at + 1) * height, :] = source[rows, :]
+        target = slice(at * height, (at + 1) * height)
+        for index in range(len(among)):
+            if source_count == len(among):
+                near_ref[index, target, :] = sources[index][rows, :]
+                continue
+            for which in range(2):
+
+                @pl.when(ring_start == which)
+                def _():
+                    near_ref[index, target, :] = sources[which * len(among) + index][rows, :]
+
         outs[at][...] = starts[at][...] if starts else jnp.zeros_like(outs[at])
 
     def one_slot(slot, carry):
@@ -109,9 +120,9 @@
     slots, depth, width = integrals.shape
     height = blocks[0].shape[0] // 4
     outs = (jax.ShapeDtypeStruct((height, width), jnp.float32),) * len(flips)
-    used = 2 + len(among) + len(starts)
+    used = 2 + len(blocks) + len(starts)
     return call(
-        lambda *refs: ladder_kernel(among, flips, *refs[:used], *refs[used + len(after) :]),
+        lambda *refs: ladder_kernel(among, flips, len(blocks), *refs[:used], *refs[used + len(after) :]),
         outs,
         [SMEM] + [VMEM] * (used - 1) + [ANY] * len(after),
         (VMEM,) * len(flips),
@@ -135,16 +146,24 @@
     code_ref[len(marks) * height :, :] = tail.astype(jnp.int32).astype(jnp.int16)
 
 
-def finish_kernel(mine_ref, arrived_ref, code_ref, occ_ref, vir_ref, out_ref):
+def finish_kernel(mine_ref, arrived_ref, code_ref, occ_ref, vir_ref, out_hbm, out_ref, sems):
     height, width = out_ref.shape
-    chunks = width // 128
+    chunks, parts = width // 128, sems.shape[0]
     marks = code_ref[chunks * height :, :].astype(jnp.int32).astype(jnp.float32)
     scales = jnp.exp2(marks * (1.0 / LOG_STEPS)) * (1.0 / LEVELS)
-    for chunk in range(chunks):
-        columns = slice(chunk * 128, (chunk + 1) * 128)
-        other = code_ref[chunk * height : (chunk + 1) * height, :].astype(jnp.int32).astype(jnp.float32)
-        total = mine_ref[:, columns] + arrived_ref[:, columns] + other * scales[chunk : chunk + 1, :]
-        out_ref[:, columns] = total / (vir_ref[:, columns] - occ_ref[...])
+    copies = []
+    for part in range(parts):
+        rows = slice(part * height // parts, (part + 1) * height // parts)
+        for chunk in range(chunks):
+            columns = slice(chunk * 128, (chunk + 1) * 128)
+            coded = slice(chunk * height + rows.start, chunk * height + rows.stop)
+            other = code_ref[coded, :].astype(jnp.int32).astype(jnp.float32)
+            total = mine_ref[rows, columns] + arrived_ref[rows, columns] + other * scales[chunk : chunk + 1, :]
+            out_ref[rows, columns] = total / (vir_ref[:, columns] - occ_ref[rows, :])
+        copies.append(pltpu.make_async_copy(out_ref.at[rows, :], out_hbm.at[rows, :], sems.at[part]))
+        copies[-1].start()
+    for copy in copies:
+        copy.wait()
 
 
 def to_other_core(value):
@@ -159,11 +178,14 @@
     own = amplitudes[0]
     height = own.shape[0] // lax.axis_size("grp")
     slots, depth, width = integrals.shape
-    arrived = {step: shifted(own, "blk", -step) for step in (1, -1)}
+    blocks = range(lax.axis_size("blk"))
+    starts_ring = [block for block in blocks if block % RING == 0]
+    below, above = shifted(own, 1), shifted(own, -1)
+    far_below_start = shifted(own, 2, starts_ring)
     plan, own_here, integrals_here = call(
         fetch_kernel,
         (
-            jax.ShapeDtypeStruct((slots + 2,), jnp.int32),
+            jax.ShapeDtypeStruct((slots + 3,), jnp.int32),
             jax.ShapeDtypeStruct(own.shape, own.dtype),
             jax.ShapeDtypeStruct(integrals.shape, integrals.dtype),
         ),
@@ -173,13 +195,12 @@
         0,
         integrals.size * 2,
     )(*[pltpu.with_memory_space_constraint(x, pltpu.HBM) for x in (cd_index, live_blocks, own, integrals)])
-    arrived[1] = gated(arrived[1], plan)
-    arrived[-1] = gated(arrived[-1], plan)
-    arrived[-2] = shifted(arrived[-1], "blk", 1)
-    arrived[2] = shifted(arrived[1], "blk", -1)
-    blocks = [arrived[step] if step else own_here for step in range(-REACH, REACH + 1)]
+    below, above = gated(below, plan), gated(above, plan)
+    far_below = shifted(below, 1, [block for block in blocks if block % RING])
+    far_above = shifted(above, -1)
     close, distant = (1, 3, 2), (0, 4)
-    close_blocks, distant_blocks = [blocks[at] for at in close], [blocks[at] for at in distant]
+    close_blocks = [below, above, own_here]
+    distant_blocks = [far_below, far_above, far_below_start, far_above]
     first = ladder(
         close, (FAR_SEND, FAR_MINE, NEAR_SEND, NEAR_MINE), plan, integrals_here, close_blocks
     )
@@ -195,8 +216,15 @@
         distant, (NEAR_SEND, NEAR_MINE), plan, integrals_here, distant_blocks, first[2:], (code,)
     )
     near_arrived = to_other_core(near_send)
+    out_shape = jax.ShapeDtypeStruct((height, width), jnp.float32)
     out = call(
-        finish_kernel, jax.ShapeDtypeStruct((height, width), jnp.float32), [VMEM] * 5, VMEM, (), 0, 1 << 20
+        finish_kernel,
+        out_shape,
+        [VMEM] * 5,
+        ANY,
+        [pltpu.VMEM(out_shape.shape, out_shape.dtype), pltpu.SemaphoreType.DMA((4,))],
+        0,
+        1 << 20,
     )(near_mine, near_arrived, code_arrived, occ_energy[:, None], vir_energy)
     return out[None]
 

time: 54.5 us -> 54.1 us (level)
  starting transfers between devices: 38 us -> 39 us
  waiting for transfers between devices: 6.02 us -> 5.07 us
    ppermute x4 -> x5, starting transfers between devices: 26.6 us -> 27.5 us  [shifted(): lax.ppermute(value, 'blk', [pair for pair in pairs if targets is None or...]
    ppermute x4 -> x5, waiting for transfers between devices: 3.28 us -> 2.36 us  [shifted(): lax.ppermute(value, 'blk', [pair for pair in pairs if targets is None or...]
  transfers between devices with their start and end apart: 7 -> 8, of which waited for: 5 -> 4; matrix products, arithmetic and copies ran while one was open for 0% -> 0% of each run, Pallas kernels for 14% -> 13%
where the time goes in v4:
time: 54.1 us; the launch traced here: 53.8 us
  starting transfers between devices  39 us (72%)
  Pallas kernels  9.47 us (18%)
  waiting for transfers between devices  5.07 us (9%)
    ppermute x5, starting transfers between devices, shifted(): lax.ppermute(value, 'blk', [pair for pair in pairs if targets is None or...  27.5 us
    ppermute x2, starting transfers between devices, to_other_core(): return lax.ppermute(value, 'grp', [(0, 1), (1, 0), (2, 3), (3, 2)])  6.94 us
    pallas_call x4, Pallas kernels, ladder(): call(lambda *refs: ladder_kernel(among, flips, len(blocks), *refs[:used],...  5.46 us
    ppermute x1, starting transfers between devices, to_other_chip(): return lax.ppermute(value, 'grp', [(0, 2), (1, 3), (2, 0), (3, 1)])  4.53 us
    pallas_call x1, Pallas kernels, body(): call(fetch_kernel, (jax.ShapeDtypeStruct((slots + 3,), jnp.int32), jax.Sh...  2.91 us
    ppermute x1, waiting for transfers between devices, to_other_chip(): return lax.ppermute(value, 'grp', [(0, 2), (1, 3), (2, 0), (3, 1)])  2.39 us
    ppermute x5, waiting for transfers between devices, shifted(): lax.ppermute(value, 'blk', [pair for pair in pairs if targets is None or...  2.36 us
  transfers between devices with their start and end apart: 8, of which 4 were waited for; matrix products, arithmetic and copies ran while one was open for 0% of the time, Pallas kernels for 13%

profile of v4, /device:TPU:1, one launch (start us, length us, event | category | flops | bytes accessed | tf_op | source)
XLA Modules:
  0.0 53.8 jit_solution(343898273915142321)
XLA Ops:
  0.0 4.4 %collective-permute-start = (bf16[512,256]{1,0:T(8,128)(2,1)}, bf16[512,256]{1,0:T(8,128)(2,1)S(1)}, u32[]{:S(2)}, u32[]{:S(2)}) collective-permute-start(bf16[512,256]{1,0:T(8,128)(2,1)} %bitcast.3), channel_id=1, source_target_pairs={{0,4},{4,8},{8,12},{12,16},{16,20},{20,24},{24,28},{28,32},{32,36}... | collective-permute-start | bytes 786440 | tf_op jit(solution)/shard_map/ppermute | solution.py:24
  4.4 12.7 %collective-permute-start.2 = (bf16[512,256]{1,0:T(8,128)(2,1)}, bf16[512,256]{1,0:T(8,128)(2,1)S(1)}, u32[]{:S(2)}, u32[]{:S(2)}) collective-permute-start(bf16[512,256]{1,0:T(8,128)(2,1)} %bitcast.4), channel_id=1, source_target_pairs={{0,508},{4,0},{8,4},{12,8},{16,12},{20,16},{24,20},{28,24},{32,28}... | collective-permute-start | bytes 786440 | tf_op jit(solution)/shard_map/ppermute | solution.py:24
  17.1 1.3 %collective-permute-start.4 = (bf16[512,256]{1,0:T(8,128)(2,1)}, bf16[512,256]{1,0:T(8,128)(2,1)S(1)}, u32[]{:S(2)}, u32[]{:S(2)}) collective-permute-start(bf16[512,256]{1,0:T(8,128)(2,1)} %bitcast.5), channel_id=1, source_target_pairs={{56,64},{120,128},{184,192},{248,256},{312,320},{376,384},{440,448... | collective-permute-start | bytes 786440 | tf_op jit(solution)/shard_map/ppermute | solution.py:24
  18.4 2.9 %shard_map.64 = (s32[11]{0:T(128)S(1)}, bf16[512,256]{1,0:T(8,128)(2,1)S(1)}, bf16[8,256,1024]{2,1,0:T(8,128)(2,1)S(1)}) custom-call(s32[1024]{0:T(1024)} %cd_hbm.1, s32[128]{0:T(128)} %live_hbm.1, bf16[512,256]{1,0:T(8,128)(2,1)} %bitcast.6, bf16[8,256,1024]{2,1,0:T(8,128)(2,1)} %integrals_hbm.1), custom_call_target="tpu_custom_call" | custom-call | bytes 4194304 | tf_op jit(solution)/shard_map/pallas_call | solution.py:185
  21.3 0.1 collective-permute-done.value_ref
  21.4 1.3 %collective-permute-start.1 = (bf16[512,256]{1,0:T(8,128)(2,1)S(1)}, bf16[512,256]{1,0:T(8,128)(2,1)S(1)}, u32[]{:S(2)}, u32[]{:S(2)}) collective-permute-start(bf16[512,256]{1,0:T(8,128)(2,1)S(1)} %shard_map.65.refs_2_), channel_id=1, source_target_pairs={{0,4},{4,8},{8,12},{12,16},{16,20},{20,24},{24,28},{28,32},{32,36}... | collective-permute-start | bytes 786440 | tf_op jit(solution)/shard_map/ppermute | solution.py:24
  22.7 0.0 collective-permute-done.2.value_ref
  22.7 7.9 %collective-permute-start.3 = (bf16[512,256]{1,0:T(8,128)(2,1)S(1)}, bf16[512,256]{1,0:T(8,128)(2,1)S(1)}, u32[]{:S(2)}, u32[]{:S(2)}) collective-permute-start(bf16[512,256]{1,0:T(8,128)(2,1)S(1)} %shard_map.66.refs_3_), channel_id=1, source_target_pairs={{0,508},{4,0},{8,4},{12,8},{16,12},{20,16},{24,20},{28,24},{32,28}... | collective-permute-start | bytes 786440 | tf_op jit(solution)/shard_map/ppermute | solution.py:24
  30.6 1.7 %shard_map.67 = (f32[128,1024]{1,0:T(8,128)S(1)}, f32[128,1024]{1,0:T(8,128)S(1)}, f32[128,1024]{1,0:T(8,128)S(1)}, f32[128,1024]{1,0:T(8,128)S(1)}) custom-call(s32[11]{0:T(128)S(1)} %get-tuple-element.14.token_ref.refs_0_, bf16[8,256,1024]{2,1,0:T(8,128)(2,1)S(1)} %get-tuple-element.15.refs_1_, bf16[512,256]{1,0:T(8,128)(2,1)S(1)} %shard_map.65.refs_2_, ...), custom_call_target="tpu_custom_call" | custom-call | flops 805306368 | tf_op jit(solution)/shard_map/pallas_call | solution.py:124
  32.3 0.0 collective-permute-done.4.refs_4_
  32.3 0.0 collective-permute-done.1.refs_2_
  32.3 2.3 %collective-permute-done.3.refs_3_.refs_5_ = bf16[512,256]{1,0:T(8,128)(2,1)S(1)} collective-permute-done((bf16[512,256]{1,0:T(8,128)(2,1)S(1)}, bf16[512,256]{1,0:T(8,128)(2,1)S(1)}, u32[]{:S(2)}, u32[]{:S(2)}) %collective-permute-start.3) | collective-permute-done | bytes 262176 | tf_op jit(solution)/shard_map/ppermute | solution.py:24
  34.6 1.2 %shard_map.68.refs_7_ = f32[128,1024]{1,0:T(8,128)S(1)} custom-call(s32[11]{0:T(128)S(1)} %get-tuple-element.14.token_ref.refs_0_, bf16[8,256,1024]{2,1,0:T(8,128)(2,1)S(1)} %get-tuple-element.15.refs_1_, bf16[512,256]{1,0:T(8,128)(2,1)S(1)} %collective-permute-done.1.refs_2_, bf16[512,256]{1,0:T(8,128)(2,1)S(1)} %collective-permute-done.3.refs_3_.refs_5_, ...), custom_call_target="tpu_custom_call" | custom-call | flops 201326592 | tf_op jit(solution)/shard_map/pallas_call | solution.py:124
  35.8 4.4 %collective-permute-start.5 = (f32[128,1024]{1,0:T(8,128)S(1)}, f32[128,1024]{1,0:T(8,128)S(1)}, u32[]{:S(2)}, u32[]{:S(2)}) collective-permute-start(f32[128,1024]{1,0:T(8,128)S(1)} %shard_map.68.refs_7_), channel_id=1, source_target_pairs={{0,1},{1,0},{2,3},{3,2},{4,5},{5,4},{6,7},{7,6},{8,9},{9,8},{10,11... | collective-permute-start | bytes 1572872 | tf_op jit(solution)/shard_map/ppermute | solution.py:170
  40.2 1.2 %shard_map.69.mine_ref = f32[128,1024]{1,0:T(8,128)S(1)} custom-call(s32[11]{0:T(128)S(1)} %get-tuple-element.14.token_ref.refs_0_, bf16[8,256,1024]{2,1,0:T(8,128)(2,1)S(1)} %get-tuple-element.15.refs_1_, bf16[512,256]{1,0:T(8,128)(2,1)S(1)} %collective-permute-done.1.refs_2_, bf16[512,256]{1,0:T(8,128)(2,1)S(1)} %collective-permute-done.3.refs_3_.refs_5_, ...), custom_call_target="tpu_custom_call" | custom-call | flops 201326592 | tf_op jit(solution)/shard_map/pallas_call | solution.py:124
  41.4 0.0 copy-start.1
  41.4 0.3 collective-permute-done.5.arrived_ref
  41.7 0.2 shard_map.70.refs_8_
  41.9 4.5 %collective-permute-start.7 = (s16[1040,128]{1,0:T(8,128)(2,1)S(1)}, s16[1040,128]{1,0:T(8,128)(2,1)S(1)}, u32[]{:S(2)}, u32[]{:S(2)}) collective-permute-start(s16[1040,128]{1,0:T(8,128)(2,1)S(1)} %shard_map.70.refs_8_), channel_id=1, source_target_pairs={{0,2},{1,3},{2,0},{3,1},{4,6},{5,7},{6,4},{7,5},{8,10},{9,11},{10,... | collective-permute-start | bytes 798728 | tf_op jit(solution)/shard_map/ppermute | solution.py:174
  46.4 1.4 %shard_map.71 = (f32[128,1024]{1,0:T(8,128)S(1)}, f32[128,1024]{1,0:T(8,128)S(1)}) custom-call(s32[11]{0:T(128)S(1)} %get-tuple-element.14.token_ref.refs_0_, bf16[8,256,1024]{2,1,0:T(8,128)(2,1)S(1)} %get-tuple-element.15.refs_1_, bf16[512,256]{1,0:T(8,128)(2,1)S(1)} %collective-permute-done.1.refs_2_, ...), custom_call_target="tpu_custom_call" | custom-call | flops 402653184 | tf_op jit(solution)/shard_map/pallas_call | solution.py:124
  47.8 2.6 %collective-permute-start.6 = (f32[128,1024]{1,0:T(8,128)S(1)}, f32[128,1024]{1,0:T(8,128)S(1)}, u32[]{:S(2)}, u32[]{:S(2)}) collective-permute-start(f32[128,1024]{1,0:T(8,128)S(1)} %get-tuple-element.22), channel_id=1, source_target_pairs={{0,1},{1,0},{2,3},{3,2},{4,5},{5,4},{6,7},{7,6},{8,9},{9,8},{10,11... | collective-permute-start | bytes 1572872 | tf_op jit(solution)/shard_map/ppermute | solution.py:170
  50.3 0.0 copy-done.1
  50.4 0.1 copy.10.occ_ref
  50.5 0.0 copy-start
  50.5 2.4 %collective-permute-done.7.value_ref = s16[1040,128]{1,0:T(8,128)(2,1)S(1)} collective-permute-done((s16[1040,128]{1,0:T(8,128)(2,1)S(1)}, s16[1040,128]{1,0:T(8,128)(2,1)S(1)}, u32[]{:S(2)}, u32[]{:S(2)}) %collective-permute-start.7) | collective-permute-done | bytes 266272 | tf_op jit(solution)/shard_map/ppermute | solution.py:174
  52.9 0.0 collective-permute-done.6.arrived_ref
  52.9 0.0 copy-done
  52.9 0.9 %shard_map.73 = f32[128,1024]{1,0:T(8,128)} custom-call(f32[128,1024]{1,0:T(8,128)S(1)} %get-tuple-element.21.mine_ref, f32[128,1024]{1,0:T(8,128)S(1)} %collective-permute-done.6.arrived_ref, s16[1040,128]{1,0:T(8,128)(2,1)S(1)} %shard_map.72.code_ref, f32[128,1]{1,0:T(8,128)S(1)} %copy.10.occ_ref, f32[1,1024]{1,0:T(1,128)S(1)} %copy-done), custom_call_target="tpu_custom_call" | custom-call | bytes 1048576 | tf_op jit(solution)/shard_map/pallas_call | solution.py:220
  (3 shorter events, 0.0 us)
Async XLA Ops:
  0.0 21.4 %collective-permute-start = (bf16[512,256]{1,0:T(8,128)(2,1)}, bf16[512,256]{1,0:T(8,128)(2,1)S(1)}, u32[]{:S(2)}, u32[]{:S(2)}) collective-permute-start(bf16[512,256]{1,0:T(8,128)(2,1)} %bitcast.3), channel_id=1, source_target_pairs={{0,4},{4,8},{8,12},{12,16},{16,20},{20,24},{24,28},{28,32},{32,36}... | collective-permute-start | bytes 786440 | tf_op jit(solution)/shard_map/ppermute | solution.py:24
  4.4 18.3 %collective-permute-start.2 = (bf16[512,256]{1,0:T(8,128)(2,1)}, bf16[512,256]{1,0:T(8,128)(2,1)S(1)}, u32[]{:S(2)}, u32[]{:S(2)}) collective-permute-start(bf16[512,256]{1,0:T(8,128)(2,1)} %bitcast.4), channel_id=1, source_target_pairs={{0,508},{4,0},{8,4},{12,8},{16,12},{20,16},{24,20},{28,24},{32,28}... | collective-permute-start | bytes 786440 | tf_op jit(solution)/shard_map/ppermute | solution.py:24
  17.1 15.2 %collective-permute-start.4 = (bf16[512,256]{1,0:T(8,128)(2,1)}, bf16[512,256]{1,0:T(8,128)(2,1)S(1)}, u32[]{:S(2)}, u32[]{:S(2)}) collective-permute-start(bf16[512,256]{1,0:T(8,128)(2,1)} %bitcast.5), channel_id=1, source_target_pairs={{56,64},{120,128},{184,192},{248,256},{312,320},{376,384},{440,448... | collective-permute-start | bytes 786440 | tf_op jit(solution)/shard_map/ppermute | solution.py:24
  21.4 10.9 %collective-permute-start.1 = (bf16[512,256]{1,0:T(8,128)(2,1)S(1)}, bf16[512,256]{1,0:T(8,128)(2,1)S(1)}, u32[]{:S(2)}, u32[]{:S(2)}) collective-permute-start(bf16[512,256]{1,0:T(8,128)(2,1)S(1)} %shard_map.65.refs_2_), channel_id=1, source_target_pairs={{0,4},{4,8},{8,12},{12,16},{16,20},{20,24},{24,28},{28,32},{32,36}... | collective-permute-start | bytes 786440 | tf_op jit(solution)/shard_map/ppermute | solution.py:24
  22.7 11.9 %collective-permute-start.3 = (bf16[512,256]{1,0:T(8,128)(2,1)S(1)}, bf16[512,256]{1,0:T(8,128)(2,1)S(1)}, u32[]{:S(2)}, u32[]{:S(2)}) collective-permute-start(bf16[512,256]{1,0:T(8,128)(2,1)S(1)} %shard_map.66.refs_3_), channel_id=1, source_target_pairs={{0,508},{4,0},{8,4},{12,8},{16,12},{20,16},{24,20},{28,24},{32,28}... | collective-permute-start | bytes 786440 | tf_op jit(solution)/shard_map/ppermute | solution.py:24
  35.8 5.9 %collective-permute-start.5 = (f32[128,1024]{1,0:T(8,128)S(1)}, f32[128,1024]{1,0:T(8,128)S(1)}, u32[]{:S(2)}, u32[]{:S(2)}) collective-permute-start(f32[128,1024]{1,0:T(8,128)S(1)} %shard_map.68.refs_7_), channel_id=1, source_target_pairs={{0,1},{1,0},{2,3},{3,2},{4,5},{5,4},{6,7},{7,6},{8,9},{9,8},{10,11... | collective-permute-start | bytes 1572872 | tf_op jit(solution)/shard_map/ppermute | solution.py:170
  41.4 9.0 %copy-start.1 = (f32[128]{0:T(128)S(1)}, f32[128]{0:T(128)}, u32[]{:S(2)}) copy-start(f32[128]{0:T(128)} %param.10) | copy-start | bytes 1540
  41.9 11.0 %collective-permute-start.7 = (s16[1040,128]{1,0:T(8,128)(2,1)S(1)}, s16[1040,128]{1,0:T(8,128)(2,1)S(1)}, u32[]{:S(2)}, u32[]{:S(2)}) collective-permute-start(s16[1040,128]{1,0:T(8,128)(2,1)S(1)} %shard_map.70.refs_8_), channel_id=1, source_target_pairs={{0,2},{1,3},{2,0},{3,1},{4,6},{5,7},{6,4},{7,5},{8,10},{9,11},{10,... | collective-permute-start | bytes 798728 | tf_op jit(solution)/shard_map/ppermute | solution.py:174
  47.8 5.1 %collective-permute-start.6 = (f32[128,1024]{1,0:T(8,128)S(1)}, f32[128,1024]{1,0:T(8,128)S(1)}, u32[]{:S(2)}, u32[]{:S(2)}) collective-permute-start(f32[128,1024]{1,0:T(8,128)S(1)} %get-tuple-element.22), channel_id=1, source_target_pairs={{0,1},{1,0},{2,3},{3,2},{4,5},{5,4},{6,7},{7,6},{8,9},{9,8},{10,11... | collective-permute-start | bytes 1572872 | tf_op jit(solution)/shard_map/ppermute | solution.py:170
  50.5 2.4 %copy-start = (f32[1,1024]{1,0:T(1,128)S(1)}, f32[1,1024]{1,0:T(1,128)}, u32[]{:S(2)}) copy-start(f32[1,1024]{1,0:T(1,128)} %vir_ref.1) | copy-start | bytes 12292

commit v5 on v4

--- a/solution.py
+++ b/solution.py
@@ -51,7 +51,8 @@
         plan_ref[slot] = jnp.where(slot < live_ref[here], offset, -1)
     plan_ref[slots] = grp // 2
     plan_ref[slots + 1] = lax.rem(grp, 2)
-    plan_ref[slots + 2] = jnp.where(lax.rem(here, RING) == 0, 1, 0)
+    place = lax.rem(here, RING)
+    plan_ref[slots + 2] = jnp.where(place == 0, 1, jnp.where((place == RING - 1) & (lax.rem(grp, 2) == 0), 2, 0))
     copies[2].wait()
     copies[3].wait()
 
@@ -74,7 +75,7 @@
     starts = rest[: len(rest) - 1 - len(flips)]
     slots, depth, width = integrals_ref.shape
     height = outs[0].shape[0]
-    high, core, ring_start = plan_ref[slots], plan_ref[slots + 1], plan_ref[slots + 2]
+    high, core, edge = plan_ref[slots], plan_ref[slots + 1], plan_ref[slots + 2]
     for at, (flip_high, flip_core) in enumerate(flips):
         block = 2 * (1 - high if flip_high else high) + (1 - core if flip_core else core)
         rows = pl.ds(pl.multiple_of(block * height, height), height)
@@ -83,9 +84,9 @@
             if source_count == len(among):
                 near_ref[index, target, :] = sources[index][rows, :]
                 continue
-            for which in range(2):
-
-                @pl.when(ring_start == which)
+            for which in range(source_count // len(among)):
+
+                @pl.when(edge == which)
                 def _():
                     near_ref[index, target, :] = sources[which * len(among) + index][rows, :]
 
@@ -179,9 +180,16 @@
     height = own.shape[0] // lax.axis_size("grp")
     slots, depth, width = integrals.shape
     blocks = range(lax.axis_size("blk"))
-    starts_ring = [block for block in blocks if block % RING == 0]
     below, above = shifted(own, 1), shifted(own, -1)
-    far_below_start = shifted(own, 2, starts_ring)
+    far_below_start = shifted(own, 2, [block for block in blocks if block % RING == 0])
+    count, group = lax.axis_size("blk"), lax.axis_size("grp")
+    over_end = [
+        ((block + 2) % count * group + grp, block * group + grp)
+        for block in blocks
+        for grp in range(group)
+        if block % RING == RING - 1 and grp % 2 == 0
+    ]
+    far_above_end = lax.ppermute(own, ("blk", "grp"), over_end)
     plan, own_here, integrals_here = call(
         fetch_kernel,
         (
@@ -195,12 +203,17 @@
         0,
         integrals.size * 2,
     )(*[pltpu.with_memory_space_constraint(x, pltpu.HBM) for x in (cd_index, live_blocks, own, integrals)])
-    below, above = gated(below, plan), gated(above, plan)
     far_below = shifted(below, 1, [block for block in blocks if block % RING])
-    far_above = shifted(above, -1)
+    onward = [
+        ((block + 1) % count * group + grp, block * group + grp)
+        for block in blocks
+        for grp in range(group)
+        if block % RING != RING - 1 or grp % 2 != 0
+    ]
+    far_above = lax.ppermute(above, ("blk", "grp"), onward)
     close, distant = (1, 3, 2), (0, 4)
     close_blocks = [below, above, own_here]
-    distant_blocks = [far_below, far_above, far_below_start, far_above]
+    distant_blocks = [far_below, far_above, far_below_start, far_above, far_below, far_above_end]
     first = ladder(
         close, (FAR_SEND, FAR_MINE, NEAR_SEND, NEAR_MINE), plan, integrals_here, close_blocks
     )

time: 54.1 us -> 53.4 us (0.987)
  starting transfers between devices: 39 us -> 37 us
  waiting for transfers between devices: 5.07 us -> 5.84 us
    ppermute x0 -> x2, starting transfers between devices: none -> 8.54 us  [the longest x1 7.87 us: body(): far_above = lax.ppermute(above, ('blk', 'grp'), onward)]
    ppermute x5 -> x4, starting transfers between devices: 27.5 us -> 19.7 us  [shifted(): lax.ppermute(value, 'blk', [pair for pair in pairs if targets is None or...]
    ppermute x2, starting transfers between devices: 6.94 us -> 4.26 us  [to_other_core(): return lax.ppermute(value, 'grp', [(0, 1), (1, 0), (2, 3), (3, 2)])]
    ppermute x5 -> x4, waiting for transfers between devices: 2.36 us -> 2.32 us  [shifted(): lax.ppermute(value, 'blk', [pair for pair in pairs if targets is None or...]
  transfers between devices with their start and end apart: 8 -> 9, of which waited for: 4 -> 3; matrix products, arithmetic and copies ran while one was open for 0% -> 0% of each run, Pallas kernels for 13% -> 14%
where the time goes in v5:
time: 53.4 us; the launch traced here: 53.1 us
  starting transfers between devices  37 us (69%)
  Pallas kernels  9.93 us (19%)
  waiting for transfers between devices  5.84 us (11%)
    ppermute x4, starting transfers between devices, shifted(): lax.ppermute(value, 'blk', [pair for pair in pairs if targets is None or...  19.7 us
    ppermute x1, starting transfers between devices, body(): far_above = lax.ppermute(above, ('blk', 'grp'), onward)  7.87 us
    pallas_call x4, Pallas kernels, ladder(): call(lambda *refs: ladder_kernel(among, flips, len(blocks), *refs[:used],...  5.93 us
    ppermute x1, starting transfers between devices, to_other_chip(): return lax.ppermute(value, 'grp', [(0, 2), (1, 3), (2, 0), (3, 1)])  4.53 us
    ppermute x2, starting transfers between devices, to_other_core(): return lax.ppermute(value, 'grp', [(0, 1), (1, 0), (2, 3), (3, 2)])  4.26 us
    pallas_call x1, Pallas kernels, body(): call(fetch_kernel, (jax.ShapeDtypeStruct((slots + 3,), jnp.int32), jax.Sh...  2.91 us
    ppermute x1, waiting for transfers between devices, to_other_chip(): return lax.ppermute(value, 'grp', [(0, 2), (1, 3), (2, 0), (3, 1)])  2.85 us
    ppermute x4, waiting for transfers between devices, shifted(): lax.ppermute(value, 'blk', [pair for pair in pairs if targets is None or...  2.32 us
  transfers between devices with their start and end apart: 9, of which 3 were waited for; matrix products, arithmetic and copies ran while one was open for 0% of the time, Pallas kernels for 14%

profile of v5, /device:TPU:1, one launch (start us, length us, event | category | flops | bytes accessed | tf_op | source)
XLA Modules:
  0.0 53.1 jit_solution(18417484102095526559)
XLA Ops:
  0.0 4.4 %collective-permute-start = (bf16[512,256]{1,0:T(8,128)(2,1)}, bf16[512,256]{1,0:T(8,128)(2,1)S(1)}, u32[]{:S(2)}, u32[]{:S(2)}) collective-permute-start(bf16[512,256]{1,0:T(8,128)(2,1)} %bitcast.3), channel_id=1, source_target_pairs={{0,4},{4,8},{8,12},{12,16},{16,20},{20,24},{24,28},{28,32},{32,36}... | collective-permute-start | bytes 786440 | tf_op jit(solution)/shard_map/ppermute | solution.py:24
  4.4 12.7 %collective-permute-start.2 = (bf16[512,256]{1,0:T(8,128)(2,1)}, bf16[512,256]{1,0:T(8,128)(2,1)S(1)}, u32[]{:S(2)}, u32[]{:S(2)}) collective-permute-start(bf16[512,256]{1,0:T(8,128)(2,1)} %bitcast.4), channel_id=1, source_target_pairs={{0,508},{4,0},{8,4},{12,8},{16,12},{20,16},{24,20},{28,24},{32,28}... | collective-permute-start | bytes 786440 | tf_op jit(solution)/shard_map/ppermute | solution.py:24
  17.1 1.3 %collective-permute-start.4 = (bf16[512,256]{1,0:T(8,128)(2,1)}, bf16[512,256]{1,0:T(8,128)(2,1)S(1)}, u32[]{:S(2)}, u32[]{:S(2)}) collective-permute-start(bf16[512,256]{1,0:T(8,128)(2,1)} %bitcast.5), channel_id=1, source_target_pairs={{56,64},{120,128},{184,192},{248,256},{312,320},{376,384},{440,448... | collective-permute-start | bytes 786440 | tf_op jit(solution)/shard_map/ppermute | solution.py:24
  18.4 0.7 %collective-permute-start.5 = (bf16[512,256]{1,0:T(8,128)(2,1)}, bf16[512,256]{1,0:T(8,128)(2,1)S(1)}, u32[]{:S(2)}, u32[]{:S(2)}) collective-permute-start(bf16[512,256]{1,0:T(8,128)(2,1)} %bitcast.6), channel_id=1, source_target_pairs={{68,60},{70,62},{132,124},{134,126},{196,188},{198,190},{260,252},... | collective-permute-start | bytes 786440 | tf_op jit(solution)/shard_map/ppermute | solution.py:192
  19.1 2.3 %collective-permute-done.refs_2_ = bf16[512,256]{1,0:T(8,128)(2,1)S(1)} collective-permute-done((bf16[512,256]{1,0:T(8,128)(2,1)}, bf16[512,256]{1,0:T(8,128)(2,1)S(1)}, u32[]{:S(2)}, u32[]{:S(2)}) %collective-permute-start) | collective-permute-done | bytes 262176 | tf_op jit(solution)/shard_map/ppermute | solution.py:24
  21.4 1.3 %collective-permute-start.1 = (bf16[512,256]{1,0:T(8,128)(2,1)S(1)}, bf16[512,256]{1,0:T(8,128)(2,1)S(1)}, u32[]{:S(2)}, u32[]{:S(2)}) collective-permute-start(bf16[512,256]{1,0:T(8,128)(2,1)S(1)} %collective-permute-done.refs_2_), channel_id=1, source_target_pairs={{0,4},{4,8},{8,12},{12,16},{16,20},{20,24},{24,28},{28,32},{32,36}... | collective-permute-start | bytes 786440 | tf_op jit(solution)/shard_map/ppermute | solution.py:24
  22.7 0.0 collective-permute-done.2.refs_3_
  22.7 7.9 %collective-permute-start.3 = (bf16[512,256]{1,0:T(8,128)(2,1)S(1)}, bf16[512,256]{1,0:T(8,128)(2,1)S(1)}, u32[]{:S(2)}, u32[]{:S(2)}) collective-permute-start(bf16[512,256]{1,0:T(8,128)(2,1)S(1)} %collective-permute-done.2.refs_3_), channel_id=1, source_target_pairs={{4,0},{5,1},{6,2},{7,3},{8,4},{9,5},{10,6},{11,7},{12,8},{13,9},{1... | collective-permute-start | bytes 786440 | tf_op jit(solution)/shard_map/ppermute | solution.py:213
  30.6 2.9 %shard_map.64 = (s32[11]{0:T(128)S(1)}, bf16[512,256]{1,0:T(8,128)(2,1)S(1)}, bf16[8,256,1024]{2,1,0:T(8,128)(2,1)S(1)}) custom-call(s32[1024]{0:T(1024)} %cd_hbm.1, s32[128]{0:T(128)} %live_hbm.1, bf16[512,256]{1,0:T(8,128)(2,1)} %bitcast.7, bf16[8,256,1024]{2,1,0:T(8,128)(2,1)} %integrals_hbm.1), custom_call_target="tpu_custom_call" | custom-call | bytes 4194304 | tf_op jit(solution)/shard_map/pallas_call | solution.py:193
  33.5 2.2 %shard_map.65 = (f32[128,1024]{1,0:T(8,128)S(1)}, f32[128,1024]{1,0:T(8,128)S(1)}, f32[128,1024]{1,0:T(8,128)S(1)}, f32[128,1024]{1,0:T(8,128)S(1)}) custom-call(s32[11]{0:T(128)S(1)} %get-tuple-element.14.refs_0_.token_ref, bf16[8,256,1024]{2,1,0:T(8,128)(2,1)S(1)} %get-tuple-element.15.refs_1_, bf16[512,256]{1,0:T(8,128)(2,1)S(1)} %collective-permute-done.refs_2_, ...), custom_call_target="tpu_custom_call" | custom-call | flops 805306368 | tf_op jit(solution)/shard_map/pallas_call | solution.py:125
  35.7 0.0 collective-permute-done.4.refs_4_
  35.7 0.0 collective-permute-done.5.refs_7_
  35.7 0.0 collective-permute-done.1.refs_2_.refs_6_
  35.7 0.0 collective-permute-done.3.refs_3_.refs_5_
  35.7 1.2 %shard_map.66.refs_9_ = f32[128,1024]{1,0:T(8,128)S(1)} custom-call(s32[11]{0:T(128)S(1)} %get-tuple-element.14.refs_0_.token_ref, bf16[8,256,1024]{2,1,0:T(8,128)(2,1)S(1)} %get-tuple-element.15.refs_1_, bf16[512,256]{1,0:T(8,128)(2,1)S(1)} %collective-permute-done.1.refs_2_.refs_6_, bf16[512,256]{1,0:T(8,128)(2,1)S(1)} %collective-permute-done.3.refs_3_.refs_5_, ...), custom_call_target="tpu_custom_call" | custom-call | flops 201326592 | tf_op jit(solution)/shard_map/pallas_call | solution.py:125
  36.9 1.9 %collective-permute-start.6 = (f32[128,1024]{1,0:T(8,128)S(1)}, f32[128,1024]{1,0:T(8,128)S(1)}, u32[]{:S(2)}, u32[]{:S(2)}) collective-permute-start(f32[128,1024]{1,0:T(8,128)S(1)} %shard_map.66.refs_9_), channel_id=1, source_target_pairs={{0,1},{1,0},{2,3},{3,2},{4,5},{5,4},{6,7},{7,6},{8,9},{9,8},{10,11... | collective-permute-start | bytes 1572872 | tf_op jit(solution)/shard_map/ppermute | solution.py:171
  38.8 1.2 %shard_map.67.mine_ref = f32[128,1024]{1,0:T(8,128)S(1)} custom-call(s32[11]{0:T(128)S(1)} %get-tuple-element.14.refs_0_.token_ref, bf16[8,256,1024]{2,1,0:T(8,128)(2,1)S(1)} %get-tuple-element.15.refs_1_, bf16[512,256]{1,0:T(8,128)(2,1)S(1)} %collective-permute-done.1.refs_2_.refs_6_, bf16[512,256]{1,0:T(8,128)(2,1)S(1)} %collective-permute-done.3.refs_3_.refs_5_, ...), custom_call_target="tpu_custom_call" | custom-call | flops 201326592 | tf_op jit(solution)/shard_map/pallas_call | solution.py:125
  40.0 0.0 copy-start.1
  40.0 0.7 %collective-permute-done.6.arrived_ref = f32[128,1024]{1,0:T(8,128)S(1)} collective-permute-done((f32[128,1024]{1,0:T(8,128)S(1)}, f32[128,1024]{1,0:T(8,128)S(1)}, u32[]{:S(2)}, u32[]{:S(2)}) %collective-permute-start.6) | collective-permute-done | bytes 524320 | tf_op jit(solution)/shard_map/ppermute | solution.py:171
  40.7 0.2 shard_map.68.refs_10_
  40.9 4.5 %collective-permute-start.8 = (s16[1040,128]{1,0:T(8,128)(2,1)S(1)}, s16[1040,128]{1,0:T(8,128)(2,1)S(1)}, u32[]{:S(2)}, u32[]{:S(2)}) collective-permute-start(s16[1040,128]{1,0:T(8,128)(2,1)S(1)} %shard_map.68.refs_10_), channel_id=1, source_target_pairs={{0,2},{1,3},{2,0},{3,1},{4,6},{5,7},{6,4},{7,5},{8,10},{9,11},{10,... | collective-permute-start | bytes 798728 | tf_op jit(solution)/shard_map/ppermute | solution.py:175
  45.4 1.4 %shard_map.69 = (f32[128,1024]{1,0:T(8,128)S(1)}, f32[128,1024]{1,0:T(8,128)S(1)}) custom-call(s32[11]{0:T(128)S(1)} %get-tuple-element.14.refs_0_.token_ref, bf16[8,256,1024]{2,1,0:T(8,128)(2,1)S(1)} %get-tuple-element.15.refs_1_, bf16[512,256]{1,0:T(8,128)(2,1)S(1)} %collective-permute-done.1.refs_2_.refs_6_, ...), custom_call_target="tpu_custom_call" | custom-call | flops 402653184 | tf_op jit(solution)/shard_map/pallas_call | solution.py:125
  46.8 2.3 %collective-permute-start.7 = (f32[128,1024]{1,0:T(8,128)S(1)}, f32[128,1024]{1,0:T(8,128)S(1)}, u32[]{:S(2)}, u32[]{:S(2)}) collective-permute-start(f32[128,1024]{1,0:T(8,128)S(1)} %get-tuple-element.22), channel_id=1, source_target_pairs={{0,1},{1,0},{2,3},{3,2},{4,5},{5,4},{6,7},{7,6},{8,9},{9,8},{10,11... | collective-permute-start | bytes 1572872 | tf_op jit(solution)/shard_map/ppermute | solution.py:171
  49.2 0.0 copy-done.1
  49.2 0.1 copy.8.occ_ref
  49.3 0.0 copy-start
  49.3 2.8 %collective-permute-done.8.value_ref = s16[1040,128]{1,0:T(8,128)(2,1)S(1)} collective-permute-done((s16[1040,128]{1,0:T(8,128)(2,1)S(1)}, s16[1040,128]{1,0:T(8,128)(2,1)S(1)}, u32[]{:S(2)}, u32[]{:S(2)}) %collective-permute-start.8) | collective-permute-done | bytes 266272 | tf_op jit(solution)/shard_map/ppermute | solution.py:175
  52.1 0.0 collective-permute-done.7.arrived_ref
  52.1 0.0 copy-done
  52.1 0.9 %shard_map.71 = f32[128,1024]{1,0:T(8,128)} custom-call(f32[128,1024]{1,0:T(8,128)S(1)} %get-tuple-element.21.mine_ref, f32[128,1024]{1,0:T(8,128)S(1)} %collective-permute-done.7.arrived_ref, s16[1040,128]{1,0:T(8,128)(2,1)S(1)} %shard_map.70.code_ref, f32[128,1]{1,0:T(8,128)S(1)} %copy.8.occ_ref, f32[1,1024]{1,0:T(1,128)S(1)} %copy-done), custom_call_target="tpu_custom_call" | custom-call | bytes 1048576 | tf_op jit(solution)/shard_map/pallas_call | solution.py:233
  (1 shorter events, 0.0 us)
Async XLA Ops:
  0.0 21.4 %collective-permute-start = (bf16[512,256]{1,0:T(8,128)(2,1)}, bf16[512,256]{1,0:T(8,128)(2,1)S(1)}, u32[]{:S(2)}, u32[]{:S(2)}) collective-permute-start(bf16[512,256]{1,0:T(8,128)(2,1)} %bitcast.3), channel_id=1, source_target_pairs={{0,4},{4,8},{8,12},{12,16},{16,20},{20,24},{24,28},{28,32},{32,36}... | collective-permute-start | bytes 786440 | tf_op jit(solution)/shard_map/ppermute | solution.py:24
  4.4 18.3 %collective-permute-start.2 = (bf16[512,256]{1,0:T(8,128)(2,1)}, bf16[512,256]{1,0:T(8,128)(2,1)S(1)}, u32[]{:S(2)}, u32[]{:S(2)}) collective-permute-start(bf16[512,256]{1,0:T(8,128)(2,1)} %bitcast.4), channel_id=1, source_target_pairs={{0,508},{4,0},{8,4},{12,8},{16,12},{20,16},{24,20},{28,24},{32,28}... | collective-permute-start | bytes 786440 | tf_op jit(solution)/shard_map/ppermute | solution.py:24
  17.1 18.6 %collective-permute-start.4 = (bf16[512,256]{1,0:T(8,128)(2,1)}, bf16[512,256]{1,0:T(8,128)(2,1)S(1)}, u32[]{:S(2)}, u32[]{:S(2)}) collective-permute-start(bf16[512,256]{1,0:T(8,128)(2,1)} %bitcast.5), channel_id=1, source_target_pairs={{56,64},{120,128},{184,192},{248,256},{312,320},{376,384},{440,448... | collective-permute-start | bytes 786440 | tf_op jit(solution)/shard_map/ppermute | solution.py:24
  18.4 17.3 %collective-permute-start.5 = (bf16[512,256]{1,0:T(8,128)(2,1)}, bf16[512,256]{1,0:T(8,128)(2,1)S(1)}, u32[]{:S(2)}, u32[]{:S(2)}) collective-permute-start(bf16[512,256]{1,0:T(8,128)(2,1)} %bitcast.6), channel_id=1, source_target_pairs={{68,60},{70,62},{132,124},{134,126},{196,188},{198,190},{260,252},... | collective-permute-start | bytes 786440 | tf_op jit(solution)/shard_map/ppermute | solution.py:192
  21.4 14.3 %collective-permute-start.1 = (bf16[512,256]{1,0:T(8,128)(2,1)S(1)}, bf16[512,256]{1,0:T(8,128)(2,1)S(1)}, u32[]{:S(2)}, u32[]{:S(2)}) collective-permute-start(bf16[512,256]{1,0:T(8,128)(2,1)S(1)} %collective-permute-done.refs_2_), channel_id=1, source_target_pairs={{0,4},{4,8},{8,12},{12,16},{16,20},{20,24},{24,28},{28,32},{32,36}... | collective-permute-start | bytes 786440 | tf_op jit(solution)/shard_map/ppermute | solution.py:24
  22.7 13.0 %collective-permute-start.3 = (bf16[512,256]{1,0:T(8,128)(2,1)S(1)}, bf16[512,256]{1,0:T(8,128)(2,1)S(1)}, u32[]{:S(2)}, u32[]{:S(2)}) collective-permute-start(bf16[512,256]{1,0:T(8,128)(2,1)S(1)} %collective-permute-done.2.refs_3_), channel_id=1, source_target_pairs={{4,0},{5,1},{6,2},{7,3},{8,4},{9,5},{10,6},{11,7},{12,8},{13,9},{1... | collective-permute-start | bytes 786440 | tf_op jit(solution)/shard_map/ppermute | solution.py:213
  36.9 3.8 %collective-permute-start.6 = (f32[128,1024]{1,0:T(8,128)S(1)}, f32[128,1024]{1,0:T(8,128)S(1)}, u32[]{:S(2)}, u32[]{:S(2)}) collective-permute-start(f32[128,1024]{1,0:T(8,128)S(1)} %shard_map.66.refs_9_), channel_id=1, source_target_pairs={{0,1},{1,0},{2,3},{3,2},{4,5},{5,4},{6,7},{7,6},{8,9},{9,8},{10,11... | collective-permute-start | bytes 1572872 | tf_op jit(solution)/shard_map/ppermute | solution.py:171
  40.0 9.1 %copy-start.1 = (f32[128]{0:T(128)S(1)}, f32[128]{0:T(128)}, u32[]{:S(2)}) copy-start(f32[128]{0:T(128)} %param.10) | copy-start | bytes 1540
  40.9 11.3 %collective-permute-start.8 = (s16[1040,128]{1,0:T(8,128)(2,1)S(1)}, s16[1040,128]{1,0:T(8,128)(2,1)S(1)}, u32[]{:S(2)}, u32[]{:S(2)}) collective-permute-start(s16[1040,128]{1,0:T(8,128)(2,1)S(1)} %shard_map.68.refs_10_), channel_id=1, source_target_pairs={{0,2},{1,3},{2,0},{3,1},{4,6},{5,7},{6,4},{7,5},{8,10},{9,11},{10,... | collective-permute-start | bytes 798728 | tf_op jit(solution)/shard_map/ppermute | solution.py:175
  46.8 5.3 %collective-permute-start.7 = (f32[128,1024]{1,0:T(8,128)S(1)}, f32[128,1024]{1,0:T(8,128)S(1)}, u32[]{:S(2)}, u32[]{:S(2)}) collective-permute-start(f32[128,1024]{1,0:T(8,128)S(1)} %get-tuple-element.22), channel_id=1, source_target_pairs={{0,1},{1,0},{2,3},{3,2},{4,5},{5,4},{6,7},{7,6},{8,9},{9,8},{10,11... | collective-permute-start | bytes 1572872 | tf_op jit(solution)/shard_map/ppermute | solution.py:171
  49.3 2.9 %copy-start = (f32[1,1024]{1,0:T(1,128)S(1)}, f32[1,1024]{1,0:T(1,128)}, u32[]{:S(2)}) copy-start(f32[1,1024]{1,0:T(1,128)} %vir_ref.1) | copy-start | bytes 12292

commit v6 on v5

--- a/solution.py
+++ b/solution.py
@@ -40,8 +40,13 @@
 def fetch_kernel(cd_hbm, live_hbm, own_hbm, integrals_hbm, plan_ref, own_ref, integrals_ref, cd_ref, live_ref, sems):
     pairs = [(cd_hbm, cd_ref), (live_hbm, live_ref), (own_hbm, own_ref), (integrals_hbm, integrals_ref)]
     copies = [pltpu.make_async_copy(source, target, sems.at[at]) for at, (source, target) in enumerate(pairs)]
-    for copy in copies:
+    for copy in copies[:3]:
         copy.start()
+
+    @pl.when(lax.rem(lax.axis_index("grp"), 2) == 1)
+    def _():
+        copies[3].start()
+
     copies[0].wait()
     copies[1].wait()
     here, grp = lax.axis_index("blk"), lax.axis_index("grp")
@@ -54,7 +59,18 @@
     place = lax.rem(here, RING)
     plan_ref[slots + 2] = jnp.where(place == 0, 1, jnp.where((place == RING - 1) & (lax.rem(grp, 2) == 0), 2, 0))
     copies[2].wait()
-    copies[3].wait()
+
+    @pl.when(lax.rem(lax.axis_index("grp"), 2) == 1)
+    def _():
+        copies[3].wait()
+
+
+def fetch_late_kernel(held_ref, integrals_hbm, after_ref, integrals_ref, sem):
+    @pl.when(lax.rem(lax.axis_index("grp"), 2) == 0)
+    def _():
+        copy = pltpu.make_async_copy(integrals_hbm, integrals_ref, sem)
+        copy.start()
+        copy.wait()
 
 
 def gated(value, token, flops=0):
@@ -203,6 +219,7 @@
         0,
         integrals.size * 2,
     )(*[pltpu.with_memory_space_constraint(x, pltpu.HBM) for x in (cd_index, live_blocks, own, integrals)])
+    below, above = gated(below, plan), gated(above, plan)
     far_below = shifted(below, 1, [block for block in blocks if block % RING])
     onward = [
         ((block + 1) % count * group + grp, block * group + grp)
@@ -211,6 +228,16 @@
         if block % RING != RING - 1 or grp % 2 != 0
     ]
     far_above = lax.ppermute(above, ("blk", "grp"), onward)
+    integrals_here = call(
+        fetch_late_kernel,
+        jax.ShapeDtypeStruct(integrals.shape, integrals.dtype),
+        [ANY, HBM, ANY],
+        ANY,
+        [pltpu.SemaphoreType.DMA],
+        0,
+        integrals.size * 2,
+        {0: 0},
+    )(integrals_here, pltpu.with_memory_space_constraint(integrals, pltpu.HBM), plan)
     close, distant = (1, 3, 2), (0, 4)
     close_blocks = [below, above, own_here]
     distant_blocks = [far_below, far_above, far_below_start, far_above, far_below, far_above_end]

time: 53.4 us -> 53.2 us (level)
  starting transfers between devices: 37 us -> 38.7 us
  waiting for transfers between devices: 5.84 us -> 4.19 us
    ppermute x2, starting transfers between devices: 4.26 us -> 6.59 us  [to_other_core(): return lax.ppermute(value, 'grp', [(0, 1), (1, 0), (2, 3), (3, 2)])]
    ppermute x4, waiting for transfers between devices: 2.32 us -> 0.01 us  [shifted(): lax.ppermute(value, 'blk', [pair for pair in pairs if targets is None or...]
    ppermute x1, waiting for transfers between devices: 0.01 us -> 1.5 us  [body(): far_above = lax.ppermute(above, ('blk', 'grp'), onward)]
    ppermute x1, starting transfers between devices: 7.87 us -> 7.22 us  [body(): far_above = lax.ppermute(above, ('blk', 'grp'), onward)]
where the time goes in v6:
time: 53.2 us; the launch traced here: 52.7 us
  starting transfers between devices  38.7 us (73%)
  Pallas kernels  9.53 us (18%)
  waiting for transfers between devices  4.19 us (8%)
    ppermute x4, starting transfers between devices, shifted(): lax.ppermute(value, 'blk', [pair for pair in pairs if targets is None or...  19.7 us
    ppermute x1, starting transfers between devices, body(): far_above = lax.ppermute(above, ('blk', 'grp'), onward)  7.22 us
    ppermute x2, starting transfers between devices, to_other_core(): return lax.ppermute(value, 'grp', [(0, 1), (1, 0), (2, 3), (3, 2)])  6.59 us
    pallas_call x4, Pallas kernels, ladder(): call(lambda *refs: ladder_kernel(among, flips, len(blocks), *refs[:used],...  5.49 us
    ppermute x1, starting transfers between devices, to_other_chip(): return lax.ppermute(value, 'grp', [(0, 2), (1, 3), (2, 0), (3, 1)])  4.53 us
    pallas_call x1, Pallas kernels, body(): call(fetch_kernel, (jax.ShapeDtypeStruct((slots + 3,), jnp.int32), jax.Sh...  2.91 us
    ppermute x1, waiting for transfers between devices, to_other_chip(): return lax.ppermute(value, 'grp', [(0, 2), (1, 3), (2, 0), (3, 1)])  2.38 us
    ppermute x1, waiting for transfers between devices, body(): far_above = lax.ppermute(above, ('blk', 'grp'), onward)  1.5 us
  transfers between devices with their start and end apart: 9, of which 3 were waited for; matrix products, arithmetic and copies ran while one was open for 0% of the time, Pallas kernels for 14%

profile of v6, /device:TPU:1, one launch (start us, length us, event | category | flops | bytes accessed | tf_op | source)
XLA Modules:
  0.0 52.7 jit_solution(16841096702088761)
XLA Ops:
  0.0 4.4 %collective-permute-start = (bf16[512,256]{1,0:T(8,128)(2,1)}, bf16[512,256]{1,0:T(8,128)(2,1)S(1)}, u32[]{:S(2)}, u32[]{:S(2)}) collective-permute-start(bf16[512,256]{1,0:T(8,128)(2,1)} %bitcast.3), channel_id=1, source_target_pairs={{0,4},{4,8},{8,12},{12,16},{16,20},{20,24},{24,28},{28,32},{32,36}... | collective-permute-start | bytes 786440 | tf_op jit(solution)/shard_map/ppermute | solution.py:24
  4.4 12.7 %collective-permute-start.2 = (bf16[512,256]{1,0:T(8,128)(2,1)}, bf16[512,256]{1,0:T(8,128)(2,1)S(1)}, u32[]{:S(2)}, u32[]{:S(2)}) collective-permute-start(bf16[512,256]{1,0:T(8,128)(2,1)} %bitcast.4), channel_id=1, source_target_pairs={{0,508},{4,0},{8,4},{12,8},{16,12},{20,16},{24,20},{28,24},{32,28}... | collective-permute-start | bytes 786440 | tf_op jit(solution)/shard_map/ppermute | solution.py:24
  17.1 1.3 %collective-permute-start.4 = (bf16[512,256]{1,0:T(8,128)(2,1)}, bf16[512,256]{1,0:T(8,128)(2,1)S(1)}, u32[]{:S(2)}, u32[]{:S(2)}) collective-permute-start(bf16[512,256]{1,0:T(8,128)(2,1)} %bitcast.5), channel_id=1, source_target_pairs={{56,64},{120,128},{184,192},{248,256},{312,320},{376,384},{440,448... | collective-permute-start | bytes 786440 | tf_op jit(solution)/shard_map/ppermute | solution.py:24
  18.4 0.7 %collective-permute-start.5 = (bf16[512,256]{1,0:T(8,128)(2,1)}, bf16[512,256]{1,0:T(8,128)(2,1)S(1)}, u32[]{:S(2)}, u32[]{:S(2)}) collective-permute-start(bf16[512,256]{1,0:T(8,128)(2,1)} %bitcast.6), channel_id=1, source_target_pairs={{68,60},{70,62},{132,124},{134,126},{196,188},{198,190},{260,252},... | collective-permute-start | bytes 786440 | tf_op jit(solution)/shard_map/ppermute | solution.py:208
  19.1 2.9 %shard_map.64 = (s32[11]{0:T(128)S(1)}, bf16[512,256]{1,0:T(8,128)(2,1)S(1)}, bf16[8,256,1024]{2,1,0:T(8,128)(2,1)S(1)}) custom-call(s32[1024]{0:T(1024)} %cd_hbm.1, s32[128]{0:T(128)} %live_hbm.1, bf16[512,256]{1,0:T(8,128)(2,1)} %bitcast.7, bf16[8,256,1024]{2,1,0:T(8,128)(2,1)} %integrals_hbm.3), custom_call_target="tpu_custom_call" | custom-call | bytes 4194304 | tf_op jit(solution)/shard_map/pallas_call | solution.py:209
  22.0 0.0 collective-permute-done.value_ref
  22.0 1.3 %collective-permute-start.1 = (bf16[512,256]{1,0:T(8,128)(2,1)S(1)}, bf16[512,256]{1,0:T(8,128)(2,1)S(1)}, u32[]{:S(2)}, u32[]{:S(2)}) collective-permute-start(bf16[512,256]{1,0:T(8,128)(2,1)S(1)} %shard_map.66.refs_2_), channel_id=1, source_target_pairs={{0,4},{4,8},{8,12},{12,16},{16,20},{20,24},{24,28},{28,32},{32,36}... | collective-permute-start | bytes 786440 | tf_op jit(solution)/shard_map/ppermute | solution.py:24
  23.3 0.0 collective-permute-done.2.value_ref
  23.3 7.2 %collective-permute-start.3 = (bf16[512,256]{1,0:T(8,128)(2,1)S(1)}, bf16[512,256]{1,0:T(8,128)(2,1)S(1)}, u32[]{:S(2)}, u32[]{:S(2)}) collective-permute-start(bf16[512,256]{1,0:T(8,128)(2,1)S(1)} %shard_map.67.refs_3_), channel_id=1, source_target_pairs={{4,0},{5,1},{6,2},{7,3},{8,4},{9,5},{10,6},{11,7},{12,8},{13,9},{1... | collective-permute-start | bytes 786440 | tf_op jit(solution)/shard_map/ppermute | solution.py:230
  30.6 1.7 %shard_map.68 = (f32[128,1024]{1,0:T(8,128)S(1)}, f32[128,1024]{1,0:T(8,128)S(1)}, f32[128,1024]{1,0:T(8,128)S(1)}, f32[128,1024]{1,0:T(8,128)S(1)}) custom-call(s32[11]{0:T(128)S(1)} %get-tuple-element.14.after_ref.token_ref.refs_0_, bf16[8,256,1024]{2,1,0:T(8,128)(2,1)S(1)} %shard_map.65.refs_1_, bf16[512,256]{1,0:T(8,128)(2,1)S(1)} %shard_map.66.refs_2_, ...), custom_call_target="tpu_custom_call" | custom-call | flops 805306368 | tf_op jit(solution)/shard_map/pallas_call | solution.py:141
  32.3 0.0 collective-permute-done.4.refs_4_
  32.3 0.0 collective-permute-done.5.refs_7_
  32.4 0.0 collective-permute-done.1.refs_2_.refs_6_
  32.4 1.5 %collective-permute-done.3.refs_3_.refs_5_ = bf16[512,256]{1,0:T(8,128)(2,1)S(1)} collective-permute-done((bf16[512,256]{1,0:T(8,128)(2,1)S(1)}, bf16[512,256]{1,0:T(8,128)(2,1)S(1)}, u32[]{:S(2)}, u32[]{:S(2)}) %collective-permute-start.3) | collective-permute-done | bytes 262176 | tf_op jit(solution)/shard_map/ppermute | solution.py:230
  33.9 1.2 %shard_map.69.refs_9_ = f32[128,1024]{1,0:T(8,128)S(1)} custom-call(s32[11]{0:T(128)S(1)} %get-tuple-element.14.after_ref.token_ref.refs_0_, bf16[8,256,1024]{2,1,0:T(8,128)(2,1)S(1)} %shard_map.65.refs_1_, bf16[512,256]{1,0:T(8,128)(2,1)S(1)} %collective-permute-done.1.refs_2_.refs_6_, bf16[512,256]{1,0:T(8,128)(2,1)S(1)} %collective-permute-done.3.refs_3_.refs_5_, ...), custom_call_target="tpu_custom_call" | custom-call | flops 201326592 | tf_op jit(solution)/shard_map/pallas_call | solution.py:141
  35.1 4.0 %collective-permute-start.6 = (f32[128,1024]{1,0:T(8,128)S(1)}, f32[128,1024]{1,0:T(8,128)S(1)}, u32[]{:S(2)}, u32[]{:S(2)}) collective-permute-start(f32[128,1024]{1,0:T(8,128)S(1)} %shard_map.69.refs_9_), channel_id=1, source_target_pairs={{0,1},{1,0},{2,3},{3,2},{4,5},{5,4},{6,7},{7,6},{8,9},{9,8},{10,11... | collective-permute-start | bytes 1572872 | tf_op jit(solution)/shard_map/ppermute | solution.py:187
  39.1 1.2 %shard_map.70.mine_ref = f32[128,1024]{1,0:T(8,128)S(1)} custom-call(s32[11]{0:T(128)S(1)} %get-tuple-element.14.after_ref.token_ref.refs_0_, bf16[8,256,1024]{2,1,0:T(8,128)(2,1)S(1)} %shard_map.65.refs_1_, bf16[512,256]{1,0:T(8,128)(2,1)S(1)} %collective-permute-done.1.refs_2_.refs_6_, bf16[512,256]{1,0:T(8,128)(2,1)S(1)} %collective-permute-done.3.refs_3_.refs_5_, ...), custom_call_target="tpu_custom_call" | custom-call | flops 201326592 | tf_op jit(solution)/shard_map/pallas_call | solution.py:141
  40.3 0.0 copy-start.1
  40.3 0.3 collective-permute-done.6.arrived_ref
  40.6 0.2 shard_map.71.refs_10_
  40.8 4.5 %collective-permute-start.8 = (s16[1040,128]{1,0:T(8,128)(2,1)S(1)}, s16[1040,128]{1,0:T(8,128)(2,1)S(1)}, u32[]{:S(2)}, u32[]{:S(2)}) collective-permute-start(s16[1040,128]{1,0:T(8,128)(2,1)S(1)} %shard_map.71.refs_10_), channel_id=1, source_target_pairs={{0,2},{1,3},{2,0},{3,1},{4,6},{5,7},{6,4},{7,5},{8,10},{9,11},{10,... | collective-permute-start | bytes 798728 | tf_op jit(solution)/shard_map/ppermute | solution.py:191
  45.3 1.4 %shard_map.72 = (f32[128,1024]{1,0:T(8,128)S(1)}, f32[128,1024]{1,0:T(8,128)S(1)}) custom-call(s32[11]{0:T(128)S(1)} %get-tuple-element.14.after_ref.token_ref.refs_0_, bf16[8,256,1024]{2,1,0:T(8,128)(2,1)S(1)} %shard_map.65.refs_1_, bf16[512,256]{1,0:T(8,128)(2,1)S(1)} %collective-permute-done.1.refs_2_.refs_6_, ...), custom_call_target="tpu_custom_call" | custom-call | flops 402653184 | tf_op jit(solution)/shard_map/pallas_call | solution.py:141
  46.7 2.6 %collective-permute-start.7 = (f32[128,1024]{1,0:T(8,128)S(1)}, f32[128,1024]{1,0:T(8,128)S(1)}, u32[]{:S(2)}, u32[]{:S(2)}) collective-permute-start(f32[128,1024]{1,0:T(8,128)S(1)} %get-tuple-element.22), channel_id=1, source_target_pairs={{0,1},{1,0},{2,3},{3,2},{4,5},{5,4},{6,7},{7,6},{8,9},{9,8},{10,11... | collective-permute-start | bytes 1572872 | tf_op jit(solution)/shard_map/ppermute | solution.py:187
  49.3 0.0 copy-done.1
  49.3 0.1 copy.11.occ_ref
  49.4 0.0 copy-start
  49.4 2.4 %collective-permute-done.8.value_ref = s16[1040,128]{1,0:T(8,128)(2,1)S(1)} collective-permute-done((s16[1040,128]{1,0:T(8,128)(2,1)S(1)}, s16[1040,128]{1,0:T(8,128)(2,1)S(1)}, u32[]{:S(2)}, u32[]{:S(2)}) %collective-permute-start.8) | collective-permute-done | bytes 266272 | tf_op jit(solution)/shard_map/ppermute | solution.py:191
  51.8 0.0 collective-permute-done.7.arrived_ref
  51.8 0.0 copy-done
  51.8 0.9 %shard_map.74 = f32[128,1024]{1,0:T(8,128)} custom-call(f32[128,1024]{1,0:T(8,128)S(1)} %get-tuple-element.21.mine_ref, f32[128,1024]{1,0:T(8,128)S(1)} %collective-permute-done.7.arrived_ref, s16[1040,128]{1,0:T(8,128)(2,1)S(1)} %shard_map.73.code_ref, f32[128,1]{1,0:T(8,128)S(1)} %copy.11.occ_ref, f32[1,1024]{1,0:T(1,128)S(1)} %copy-done), custom_call_target="tpu_custom_call" | custom-call | bytes 1048576 | tf_op jit(solution)/shard_map/pallas_call | solution.py:260
  (4 shorter events, 0.0 us)
Async XLA Ops:
  0.0 22.0 %collective-permute-start = (bf16[512,256]{1,0:T(8,128)(2,1)}, bf16[512,256]{1,0:T(8,128)(2,1)S(1)}, u32[]{:S(2)}, u32[]{:S(2)}) collective-permute-start(bf16[512,256]{1,0:T(8,128)(2,1)} %bitcast.3), channel_id=1, source_target_pairs={{0,4},{4,8},{8,12},{12,16},{16,20},{20,24},{24,28},{28,32},{32,36}... | collective-permute-start | bytes 786440 | tf_op jit(solution)/shard_map/ppermute | solution.py:24
  4.4 19.0 %collective-permute-start.2 = (bf16[512,256]{1,0:T(8,128)(2,1)}, bf16[512,256]{1,0:T(8,128)(2,1)S(1)}, u32[]{:S(2)}, u32[]{:S(2)}) collective-permute-start(bf16[512,256]{1,0:T(8,128)(2,1)} %bitcast.4), channel_id=1, source_target_pairs={{0,508},{4,0},{8,4},{12,8},{16,12},{20,16},{24,20},{28,24},{32,28}... | collective-permute-start | bytes 786440 | tf_op jit(solution)/shard_map/ppermute | solution.py:24
  17.1 15.3 %collective-permute-start.4 = (bf16[512,256]{1,0:T(8,128)(2,1)}, bf16[512,256]{1,0:T(8,128)(2,1)S(1)}, u32[]{:S(2)}, u32[]{:S(2)}) collective-permute-start(bf16[512,256]{1,0:T(8,128)(2,1)} %bitcast.5), channel_id=1, source_target_pairs={{56,64},{120,128},{184,192},{248,256},{312,320},{376,384},{440,448... | collective-permute-start | bytes 786440 | tf_op jit(solution)/shard_map/ppermute | solution.py:24
  18.4 14.0 %collective-permute-start.5 = (bf16[512,256]{1,0:T(8,128)(2,1)}, bf16[512,256]{1,0:T(8,128)(2,1)S(1)}, u32[]{:S(2)}, u32[]{:S(2)}) collective-permute-start(bf16[512,256]{1,0:T(8,128)(2,1)} %bitcast.6), channel_id=1, source_target_pairs={{68,60},{70,62},{132,124},{134,126},{196,188},{198,190},{260,252},... | collective-permute-start | bytes 786440 | tf_op jit(solution)/shard_map/ppermute | solution.py:208
  22.0 10.4 %collective-permute-start.1 = (bf16[512,256]{1,0:T(8,128)(2,1)S(1)}, bf16[512,256]{1,0:T(8,128)(2,1)S(1)}, u32[]{:S(2)}, u32[]{:S(2)}) collective-permute-start(bf16[512,256]{1,0:T(8,128)(2,1)S(1)} %shard_map.66.refs_2_), channel_id=1, source_target_pairs={{0,4},{4,8},{8,12},{12,16},{16,20},{20,24},{24,28},{28,32},{32,36}... | collective-permute-start | bytes 786440 | tf_op jit(solution)/shard_map/ppermute | solution.py:24
  23.3 10.5 %collective-permute-start.3 = (bf16[512,256]{1,0:T(8,128)(2,1)S(1)}, bf16[512,256]{1,0:T(8,128)(2,1)S(1)}, u32[]{:S(2)}, u32[]{:S(2)}) collective-permute-start(bf16[512,256]{1,0:T(8,128)(2,1)S(1)} %shard_map.67.refs_3_), channel_id=1, source_target_pairs={{4,0},{5,1},{6,2},{7,3},{8,4},{9,5},{10,6},{11,7},{12,8},{13,9},{1... | collective-permute-start | bytes 786440 | tf_op jit(solution)/shard_map/ppermute | solution.py:230
  35.1 5.5 %collective-permute-start.6 = (f32[128,1024]{1,0:T(8,128)S(1)}, f32[128,1024]{1,0:T(8,128)S(1)}, u32[]{:S(2)}, u32[]{:S(2)}) collective-permute-start(f32[128,1024]{1,0:T(8,128)S(1)} %shard_map.69.refs_9_), channel_id=1, source_target_pairs={{0,1},{1,0},{2,3},{3,2},{4,5},{5,4},{6,7},{7,6},{8,9},{9,8},{10,11... | collective-permute-start | bytes 1572872 | tf_op jit(solution)/shard_map/ppermute | solution.py:187
  40.3 9.0 %copy-start.1 = (f32[128]{0:T(128)S(1)}, f32[128]{0:T(128)}, u32[]{:S(2)}) copy-start(f32[128]{0:T(128)} %param.10) | copy-start | bytes 1540
  40.8 11.0 %collective-permute-start.8 = (s16[1040,128]{1,0:T(8,128)(2,1)S(1)}, s16[1040,128]{1,0:T(8,128)(2,1)S(1)}, u32[]{:S(2)}, u32[]{:S(2)}) collective-permute-start(s16[1040,128]{1,0:T(8,128)(2,1)S(1)} %shard_map.71.refs_10_), channel_id=1, source_target_pairs={{0,2},{1,3},{2,0},{3,1},{4,6},{5,7},{6,4},{7,5},{8,10},{9,11},{10,... | collective-permute-start | bytes 798728 | tf_op jit(solution)/shard_map/ppermute | solution.py:191
  46.7 5.1 %collective-permute-start.7 = (f32[128,1024]{1,0:T(8,128)S(1)}, f32[128,1024]{1,0:T(8,128)S(1)}, u32[]{:S(2)}, u32[]{:S(2)}) collective-permute-start(f32[128,1024]{1,0:T(8,128)S(1)} %get-tuple-element.22), channel_id=1, source_target_pairs={{0,1},{1,0},{2,3},{3,2},{4,5},{5,4},{6,7},{7,6},{8,9},{9,8},{10,11... | collective-permute-start | bytes 1572872 | tf_op jit(solution)/shard_map/ppermute | solution.py:187
  49.4 2.4 %copy-start = (f32[1,1024]{1,0:T(1,128)S(1)}, f32[1,1024]{1,0:T(1,128)}, u32[]{:S(2)}) copy-start(f32[1,1024]{1,0:T(1,128)} %vir_ref.1) | copy-start | bytes 12292
